TPU v7x, 256 devices: a whole 4x4x8 slice. The times are simulated.
256 devices in a mesh: ctx: 32 (over x, z), head: 8 (over y, core).
Axes of the slice: x: 4, y: 4, z: 8, core: 2. Of those that a mesh axis runs over, the one named last changes fastest.
Arguments:
- keys: bfloat16 [2, 262144, 8, 128], P(None, 'ctx', 'head'), may hold values from -6.5 to 6.5
- values: bfloat16 [2, 262144, 8, 128], P(None, 'ctx', 'head'), may hold values from -6 to 6
- queries: bfloat16 [2, 2048, 64, 128], P(None, 'ctx', 'head'), may hold values from -14 to 14
- keep_blocks: int32 [2, 8, 512], P(None, 'head'), may hold values from 0 to 2047, as said below
- block_owner: int32 [2, 8, 512], P(None, 'head'), may hold values from 0 to 31, as said below
Outputs:
- pooled_mass: float32 [2, 8, 262144], P(None, 'head', 'ctx')
- shared_mass: float32 [2, 262144], P(None, 'ctx')
- compact_keys: bfloat16 [2, 8, 65536, 128], P(None, 'head', 'ctx')
- compact_values: bfloat16 [2, 8, 65536, 128], P(None, 'head', 'ctx')
- kept_mass: bfloat16 [2, 8, 512], P(None, 'head', 'ctx')
Inputs may be any that keep to these rules, and one draw needn't show every extreme that they name: `keep_blocks`: for each layer and KV head, 512 distinct block indices in increasing order; block b holds positions b * 128 to b * 128 + 127. Block 0 and block 2047 are always kept. `block_owner`: for each layer and KV head every owner receives exactly 16 kept blocks, and at most 2 kept blocks of one owner lie in the same ctx shard (block // 64); some shard reaches 2 with some owner.
All inputs are finite; a program needn't handle non-finite values.
Results may differ from a plain program's by a relative error of at most 0.001.
Values may be sent and summed in bfloat16 or wider, within the bound.
No kernel may reach another device: no remote copies, remote signals or barrier semaphores. Data moves between devices by JAX's collectives and lax.ppermute only.
A program may use at most 128 MiB of HBM per device.

v0:
```python
import jax
import jax.numpy as jnp
from jax import lax
from jax.sharding import PartitionSpec as P

KVH = 8
BLOCK = 128
POOL = 7


def spread(x, axis, root):
    mine = lax.axis_index(axis) == root
    return lax.psum(jnp.where(mine, x, jnp.zeros_like(x)), axis)


def extended(block, sides, width):
    for axis, dim in sides:
        count = lax.axis_size(axis)
        forward = [(i, i + 1) for i in range(count - 1)]
        backward = [(target, source) for source, target in forward]
        low = lax.ppermute(
            lax.slice_in_dim(block, block.shape[dim] - width, None, axis=dim), axis, forward
        )
        high = lax.ppermute(lax.slice_in_dim(block, 0, width, axis=dim), axis, backward)
        block = jnp.concatenate([low, block, high], axis=dim)
    return block


def per_device(keys, values, queries, keep_blocks, block_owner):
    width = lax.axis_size("ctx")
    position = lax.axis_index("ctx")
    layers, shard_len, heads_here, head_dim = keys.shape
    window = queries.shape[1]
    group = queries.shape[2] // heads_here
    total_len = shard_len * width
    query_rows = window * group
    blocks_here = shard_len // BLOCK
    keep_count = keep_blocks.shape[2]
    keep_share = keep_count // width
    capacity = (blocks_here + width - 1) // width
    slot_count = width * capacity
    pairs = [(l, g) for l in range(layers) for g in range(heads_here)]
    source = keep_blocks // blocks_here
    offset = keep_blocks % blocks_here
    entry = jnp.arange(keep_count, dtype=jnp.int32)
    earlier = entry[None, :] < entry[:, None]
    same_owner = block_owner[..., :, None] == block_owner[..., None, :]
    same_source = source[..., :, None] == source[..., None, :]
    owner_rank = jnp.sum(same_owner & earlier, axis=-1)
    pair_rank = jnp.sum(same_owner & same_source & earlier, axis=-1)
    slot = block_owner * capacity + pair_rank
    send_hit = (source == position)[..., None] & (
        slot[..., None] == jnp.arange(slot_count, dtype=jnp.int32)
    )
    send_index = jnp.sum(jnp.where(send_hit, offset[..., None], 0), axis=2)
    send_valid = jnp.any(send_hit, axis=2)
    recv_hit = (block_owner == position)[..., None] & (
        owner_rank[..., None] == jnp.arange(keep_share, dtype=jnp.int32)
    )
    recv_index = jnp.sum(jnp.where(recv_hit, (source * capacity + pair_rank)[..., None], 0), axis=2)

    def pack(store):
        blocked = store.reshape(layers, blocks_here, BLOCK, heads_here, head_dim)
        picked = jnp.stack(
            [jnp.stack([blocked[l, send_index[l, 0], :, 0, :]]) for l in range(layers)]
        )
        return jnp.where(send_valid[..., None, None], picked, jnp.zeros_like(picked))

    key_parcels = pack(keys)
    value_parcels = pack(values)
    windowed = spread(queries, "ctx", width - 1)
    key_pos = position * shard_len + jnp.arange(shard_len, dtype=jnp.int32)
    query_pos = total_len - window + jnp.arange(query_rows, dtype=jnp.int32) // group
    visible = key_pos[None, :] <= query_pos[:, None]
    scale = head_dim ** (-0.5)

    def scores(l, g):
        block = windowed[l, :, g * group : (g + 1) * group, :].reshape(query_rows, head_dim)
        raw = (
            lax.dot_general(
                block,
                keys[l, :, g, :],
                (((1,), (1,)), ((), ())),
                preferred_element_type=jnp.float32,
            )
            * scale
        )
        return jnp.where(visible, raw, -1e30)

    peaks = lax.pmax(jnp.stack([jnp.max(scores(l, g), axis=1) for l, g in pairs]), "ctx")
    totals = lax.psum(
        jnp.stack(
            [
                jnp.sum(jnp.exp(scores(l, g) - peaks[index][:, None]), axis=1)
                for index, (l, g) in enumerate(pairs)
            ]
        ),
        "ctx",
    )
    factor = total_len / query_rows
    mass_list = []
    for index, (l, g) in enumerate(pairs):
        weights = jnp.exp(scores(l, g) - peaks[index][:, None]) / totals[index][:, None]
        mass_list.append(jnp.sum(weights, axis=0) * factor)
    mass = jnp.stack(mass_list).reshape(layers, heads_here, shard_len)
    half = (POOL - 1) // 2
    padded = extended(mass, (("ctx", 2),), half)
    pooled = padded[..., 0:shard_len]
    for shift in range(1, POOL):
        pooled = pooled + padded[..., shift : shift + shard_len]
    pooled = pooled / POOL
    shared = lax.psum(jnp.sum(pooled, axis=1), "head") / KVH
    block_mass = jnp.sum(pooled.reshape(layers, heads_here, blocks_here, BLOCK), axis=3).astype(
        jnp.bfloat16
    )
    picked_mass = jnp.take_along_axis(block_mass, send_index, axis=2)
    mass_parcels = jnp.where(send_valid, picked_mass, jnp.zeros_like(picked_mass))
    key_got, value_got, mass_got = (
        lax.all_to_all(key_parcels, "ctx", split_axis=2, concat_axis=2, tiled=True),
        lax.all_to_all(value_parcels, "ctx", split_axis=2, concat_axis=2, tiled=True),
        lax.all_to_all(mass_parcels, "ctx", split_axis=2, concat_axis=2, tiled=True),
    )

    def unpack(received):
        gathered = jnp.stack([jnp.stack([received[l, 0][recv_index[l, 0]]]) for l in range(layers)])
        return gathered.reshape(layers, heads_here, keep_share * BLOCK, head_dim)

    kept_mass = jnp.take_along_axis(mass_got, recv_index, axis=2)
    return (pooled, shared, unpack(key_got), unpack(value_got), kept_mass)


def solution(mesh):
    in_specs = (
        P(None, "ctx", "head", None),
        P(None, "ctx", "head", None),
        P(None, "ctx", "head", None),
        P(None, "head", None),
        P(None, "head", None),
    )
    out_specs = (
        P(None, "head", "ctx"),
        P(None, "ctx"),
        P(None, "head", "ctx", None),
        P(None, "head", "ctx", None),
        P(None, "head", "ctx"),
    )
    return jax.shard_map(
        per_device, mesh=mesh, in_specs=in_specs, out_specs=out_specs, check_vma=False
    )
```

profile of v0, /device:TPU:2, one launch (start us, length us, event | category | flops | bytes accessed | tf_op | source)
XLA Modules:
  0.0 574.5 jit_solution(3684951221852463698)
XLA Ops:
  7.2 0.0 all-reduce.3.cloned.1.call-start
  7.2 0.7 broadcast_select_fusion
  8.0 0.0 all-reduce.3.cloned.1.call-update
  8.0 0.1 iota_compare_fusion
  8.1 0.7 copy.45
  8.8 0.7 compare_bitcast_fusion.1
  9.5 1.4 convert_reduce_fusion
  10.8 0.7 fusion.18
  11.6 0.2 select_reduce_fusion
  11.8 0.1 fusion.8
  11.9 3.2 gather_fusion.5
  15.1 4.3 gather_fusion.4
  19.4 4.4 gather_fusion.1
  23.8 4.3 gather_fusion
  28.1 0.1 copy.18
  28.2 0.1 reshape.589
  28.3 129.5 %all-reduce.3.cloned.1.call-done = bf16[2,64,8,128]{3,2,1,0:T(8,128)(2,1)} async-done(((bf16[2,64,8,128]{3,2,1,0:T(8,128)(2,1)}), bf16[2,64,8,128]{3,2,1,0:T(8,128)(2,1)}) %all-reduce.3.cloned.1.call-update) | async-done | bytes 262160 | tf_op jit(solution)/shard_map/psum | solution.py:13
  157.8 10.4 %fusion.41 = (f32[512]{0:T(512)S(1)}, f32[512,8192]{1,0:T(8,128)}) fusion(bf16[2,8192,1,128]{3,1,2,0:T(8,128)(2,1)} %param.5, bf16[2,64,8,128]{3,2,1,0:T(8,128)(2,1)} %all-reduce.3.cloned.1.call-done, s32[512]{0:T(512)S(1)} %fusion.19, s32[8192]{0:T(1024)S(1)} %iota_add_fusion), kind=kOutput, calls=%fused_computation.122 | convolution fusion | flops 1090518528 | bytes 19042304 | tf_op jit(solution)/shard_map/dot_general | solution.py:80
  168.2 0.0 copy-done.3
  168.2 7.2 %fusion.42 = (f32[512]{0:T(512)S(1)}, f32[512,8192]{1,0:T(8,128)}) fusion(bf16[2,8192,1,128]{3,1,2,0:T(8,128)(2,1)S(1)} %copy-done, bf16[2,64,8,128]{3,2,1,0:T(8,128)(2,1)S(1)} %copy-done.3, s32[512]{0:T(512)S(1)} %fusion.19, s32[8192]{0:T(1024)S(1)} %iota_add_fusion), kind=kOutput, calls=%fused_computation.123 | convolution fusion | flops 1090518528 | bytes 19042304 | tf_op jit(solution)/shard_map/dot_general | solution.py:80
  175.4 63.0 %pmax.7 = f32[2,512]{1,0:T(2,128)S(1)} all-reduce(f32[2,512]{1,0:T(2,128)S(1)} %pad_maximum_fusion.4), channel_id=1, replica_groups=mesh['ctx'=32,'head'=8] {'ctx'}, use_global_device_ids=true, to_apply=%region_3.4 | all-reduce | flops 1024 | bytes 8192 | tf_op jit(solution)/shard_map/pmax | solution.py:90
  238.5 8.1 %fusion.1 = f32[512]{0:T(512)S(1)} fusion(f32[512,8192]{1,0:T(8,128)} %get-tuple-element.28, f32[512]{0:T(512)S(1)} %bitcast.127), kind=kLoop, calls=%fused_computation.17 | loop fusion | flops 8388096 | bytes 16781312 | tf_op jit(solution)/shard_map/reduce_sum | solution.py:94
  246.6 8.1 %fusion = f32[512]{0:T(512)S(1)} fusion(f32[512,8192]{1,0:T(8,128)} %get-tuple-element.30, f32[512]{0:T(512)S(1)} %bitcast.125), kind=kLoop, calls=%fused_computation.16 | loop fusion | flops 8388096 | bytes 16781312 | tf_op jit(solution)/shard_map/reduce_sum | solution.py:94
  254.7 68.3 %psum.22 = f32[2,512]{1,0:T(2,128)S(1)} all-reduce(f32[2,512]{1,0:T(2,128)S(1)} %pad_maximum_fusion.5), channel_id=1, replica_groups=mesh['ctx'=32,'head'=8] {'ctx'}, use_global_device_ids=true, to_apply=%region_6.7 | all-reduce | flops 1024 | bytes 8192 | tf_op jit(solution)/shard_map/psum | solution.py:91
  323.0 7.5 %divide_reduce_fusion = f32[8192]{0:T(1024)S(1)} fusion(f32[512,8192]{1,0:T(8,128)} %get-tuple-element.28, f32[512]{0:T(512)S(1)} %bitcast.130, f32[512]{0:T(512)S(1)} %bitcast.128), kind=kLoop, calls=%fused_computation.14 | loop fusion | flops 12574720 | bytes 16814080 | tf_op jit(solution)/shard_map/reduce_sum | solution.py:104
  330.5 7.5 %divide_reduce_fusion.1 = f32[8192]{0:T(1024)S(1)} fusion(f32[512,8192]{1,0:T(8,128)} %get-tuple-element.30, f32[512]{0:T(512)S(1)} %bitcast.129, f32[512]{0:T(512)S(1)} %bitcast.126), kind=kLoop, calls=%fused_computation.15 | loop fusion | flops 12574720 | bytes 16814080 | tf_op jit(solution)/shard_map/reduce_sum | solution.py:104
  338.1 0.1 pad_maximum_fusion.3
  338.3 0.1 fusion.38
  338.3 7.2 %collective-permute-start.1 = (f32[2,1,3]{2,1,0:T(1,128)S(1)}, f32[2,1,3]{2,1,0:T(1,128)S(1)}, u32[]{:S(2)}, u32[]{:S(2)}) collective-permute-start(f32[2,1,3]{2,1,0:T(1,128)S(1)} %get-tuple-element.14), channel_id=1, source_target_pairs={{8,0},{16,8},{24,16},{32,24},{40,32},{48,40},{56,48},{64,56},{72,6... | collective-permute-start | bytes 80 | tf_op jit(solution)/shard_map/ppermute | solution.py:24
  345.6 1.9 collective-permute-start
  347.5 0.0 collective-permute-done.1
  347.5 6.3 %collective-permute-done = f32[2,1,3]{2,1,0:T(1,128)S(1)} collective-permute-done((f32[2,1,3]{2,1,0:T(1,128)S(1)}, f32[2,1,3]{2,1,0:T(1,128)S(1)}, u32[]{:S(2)}, u32[]{:S(2)}) %collective-permute-start) | collective-permute-done | bytes 56 | tf_op jit(solution)/shard_map/ppermute | solution.py:21
  353.8 0.9 fusion.12
  354.6 0.0 copy-start.1
  354.7 0.1 reduce_sum.109
  354.8 1.5 gather_fusion.8
  356.3 0.1 reshape.588
  356.4 0.7 copy.20
  357.1 10.8 %all-to-all-start.2 = ((bf16[2,1,64]{0,1,2:T(2,128)(2,1)}), bf16[2,1,64]{0,1,2:T(2,128)(2,1)S(1)}, u32[]{:S(2)}, u32[]{:S(2)}) async-start(bf16[2,1,64]{0,1,2:T(2,128)(2,1)} %copy.20), calls=%async_computation.2 | async-start | bytes 65536 | tf_op jit(solution)/shard_map/all_to_all | solution.py:121
  367.9 5.6 maximum_select_fusion.1
  373.5 3.5 all-to-all-done.2
  377.0 88.0 %all_to_all.15 = bf16[2,1,64,128,128]{4,3,1,0,2:T(8,128)(2,1)} all-to-all(bf16[2,1,64,128,128]{4,3,1,0,2:T(8,128)(2,1)} %get-tuple-element.16), channel_id=1, replica_groups=mesh['ctx'=32,'head'=8] {'ctx'}, dimensions={2} | all-to-all | bytes 8388608 | tf_op jit(solution)/shard_map/all_to_all | solution.py:119
  464.9 11.2 %all-to-all-start.1 = ((bf16[2,1,64,128,128]{4,3,1,0,2:T(8,128)(2,1)}), bf16[2,1,64,128,128]{4,3,1,0,2:T(8,128)(2,1)}, u32[]{:S(2)}, u32[]{:S(2)}) async-start(bf16[2,1,64,128,128]{4,3,1,0,2:T(8,128)(2,1)} %get-tuple-element.15), calls=%async_computation.1 | async-start | bytes 8388608 | tf_op jit(solution)/shard_map/all_to_all | solution.py:120
  476.2 0.0 all-reduce.5.cloned.1.call-start
  476.3 0.0 copy-done.2
  476.3 0.1 select_reduce_fusion.1
  476.4 0.1 reshape.597
  476.5 0.7 copy.44
  477.2 0.0 all-reduce.5.cloned.1.call-update
  477.2 0.1 copy.21
  477.3 0.8 gather_fusion.9
  478.1 0.1 reshape.596
  478.2 0.5 and_select_fusion.3
  478.7 67.4 %all-reduce.5.cloned.1.call-done = f32[2,8192]{1,0:T(2,128)} async-done(((f32[2,8192]{1,0:T(2,128)}), f32[2,8192]{1,0:T(2,128)}) %all-reduce.5.cloned.1.call-update) | async-done | bytes 65552 | tf_op jit(solution)/shard_map/psum | solution.py:112
  546.0 1.5 broadcast_multiply_fusion
  547.5 4.0 slice_bitcast_fusion.3
  551.6 2.2 gather_fusion.3
  553.8 0.0 all-to-all-done.1
  553.8 4.8 slice_bitcast_fusion.1
  558.6 2.2 gather_fusion.7
  560.8 1.4 gather_fusion.2
  562.3 2.2 gather_fusion.6
  564.5 2.1 pad_maximum_fusion
  566.6 1.1 pad_maximum_fusion.1
  (24 shorter events, 0.2 us)
Async XLA Ops:
  7.2 150.6 %all-reduce.3.cloned.1.call-start = ((), (), s32[]{:S(2)}) async-start(), calls=%async_computation.3 | async-start | bytes 524288 | tf_op jit(solution)/shard_map/psum | solution.py:13
  157.8 10.4 %copy-start = (bf16[2,8192,1,128]{3,1,2,0:T(8,128)(2,1)S(1)}, bf16[2,8192,1,128]{3,1,2,0:T(8,128)(2,1)}, u32[]{:S(2)}) copy-start(bf16[2,8192,1,128]{3,1,2,0:T(8,128)(2,1)} %param.5) | copy-start | bytes 12582916
  157.8 10.4 %copy-start.3 = (bf16[2,64,8,128]{3,2,1,0:T(8,128)(2,1)S(1)}, bf16[2,64,8,128]{3,2,1,0:T(8,128)(2,1)}, u32[]{:S(2)}) copy-start(bf16[2,64,8,128]{3,2,1,0:T(8,128)(2,1)} %all-reduce.3.cloned.1.call-done) | copy-start | bytes 786436
  338.3 9.2 %collective-permute-start.1 = (f32[2,1,3]{2,1,0:T(1,128)S(1)}, f32[2,1,3]{2,1,0:T(1,128)S(1)}, u32[]{:S(2)}, u32[]{:S(2)}) collective-permute-start(f32[2,1,3]{2,1,0:T(1,128)S(1)} %get-tuple-element.14), channel_id=1, source_target_pairs={{8,0},{16,8},{24,16},{32,24},{40,32},{48,40},{56,48},{64,56},{72,6... | collective-permute-start | bytes 80 | tf_op jit(solution)/shard_map/ppermute | solution.py:24
  345.6 8.2 %collective-permute-start = (f32[2,1,3]{2,1,0:T(1,128)S(1)}, f32[2,1,3]{2,1,0:T(1,128)S(1)}, u32[]{:S(2)}, u32[]{:S(2)}) collective-permute-start(f32[2,1,3]{2,1,0:T(1,128)S(1)} %get-tuple-element.13), channel_id=1, source_target_pairs={{0,8},{8,16},{16,24},{24,32},{32,40},{40,48},{48,56},{56,64},{64,7... | collective-permute-start | bytes 80 | tf_op jit(solution)/shard_map/ppermute | solution.py:21
  354.6 121.9 %copy-start.1 = (f32[2,1,8192]{2,1,0:T(1,128)}, f32[2,1,8192]{2,1,0:T(1,128)S(1)}, u32[]{:S(2)}) copy-start(f32[2,1,8192]{2,1,0:T(1,128)S(1)} %fusion.12) | copy-start | bytes 196612
  357.1 19.9 %all-to-all-start.2 = ((bf16[2,1,64]{0,1,2:T(2,128)(2,1)}), bf16[2,1,64]{0,1,2:T(2,128)(2,1)S(1)}, u32[]{:S(2)}, u32[]{:S(2)}) async-start(bf16[2,1,64]{0,1,2:T(2,128)(2,1)} %copy.20), calls=%async_computation.2 | async-start | bytes 65536 | tf_op jit(solution)/shard_map/all_to_all | solution.py:121
  464.9 11.3 %copy-start.2 = (s32[2,1,512]{2,1,0:T(1,128)S(1)}, s32[2,1,512]{2,1,0:T(1,128)}, u32[]{:S(2)}) copy-start(s32[2,1,512]{2,1,0:T(1,128)} %param.9) | copy-start | bytes 12292
  464.9 88.9 %all-to-all-start.1 = ((bf16[2,1,64,128,128]{4,3,1,0,2:T(8,128)(2,1)}), bf16[2,1,64,128,128]{4,3,1,0,2:T(8,128)(2,1)}, u32[]{:S(2)}, u32[]{:S(2)}) async-start(bf16[2,1,64,128,128]{4,3,1,0,2:T(8,128)(2,1)} %get-tuple-element.15), calls=%async_computation.1 | async-start | bytes 8388608 | tf_op jit(solution)/shard_map/all_to_all | solution.py:120
  476.2 69.8 %all-reduce.5.cloned.1.call-start = ((), (), s32[]{:S(2)}) async-start(), calls=%async_computation.4 | async-start | bytes 131072 | tf_op jit(solution)/shard_map/psum | solution.py:112
Sparse Core Ops, SparseCore 0:
  12.0 145.7 all-reduce.2
  479.9 66.0 all-reduce.4
where the time goes:
time: 575 us
  blocking collectives  219 us (38%)
  waiting for transfers between devices  207 us (36%)
  other arithmetic  47.3 us (8%)
  local copies, waits for them, and re-layouts  38.2 us (7%)
  starting transfers between devices  31.2 us (5%)
  matrix products  17.6 us (3%)
  between operations  14.3 us (2%)
    psum x1, waiting for transfers between devices, spread(): return lax.psum(jnp.where(mine, x, jnp.zeros_like(x)), axis)  129 us
    all_to_all x1, blocking collectives, per_device(): lax.all_to_all(key_parcels, 'ctx', split_axis=2, concat_axis=2, tiled=True)  88 us
    psum x1, blocking collectives, per_device(): lax.psum(jnp.stack([jnp.sum(jnp.exp(scores(l, g) - peaks[index][:, None])...  68.3 us
    psum x1, waiting for transfers between devices, per_device(): shared = lax.psum(jnp.sum(pooled, axis=1), 'head') / KVH  67.4 us
    pmax x1, blocking collectives, per_device(): lax.pmax(jnp.stack([jnp.max(scores(l, g), axis=1) for l, g in pairs]), 'c...  63 us
    dot_general x2, matrix products, scores(): lax.dot_general(block, keys[l, :, g, :], (((1,), (1,)), ((), ())), prefer...  17.6 us
    reduce_sum x2, other arithmetic, per_device(): jnp.sum(jnp.exp(scores(l, g) - peaks[index][:, None]), axis=1)  16.2 us
    gather x4, local copies, waits for them, and re-layouts, pack(): blocked[l, send_index[l, 0], :, 0, :]  16.2 us
  transfers between devices with their start and end apart: 6, of which 4 were waited for; matrix products, arithmetic and copies ran while one was open for 6% of the time, Pallas kernels for 0%

commit v1 on v0

v1 whole, which is shorter than its diff:
```python
import functools
import math
import jax
import jax.numpy as jnp
from jax import lax
from jax.experimental import pallas as pl
from jax.experimental.pallas import tpu as pltpu
from jax.sharding import PartitionSpec as P

KVH = 8
BLOCK = 128
POOL = 7
LANES = 128
TILE = 1024
NEG = -1e30
MIB = 1 << 20


def pack_kernel(index_ref, keys_ref, values_ref, after_ref, out_ref, sem):
    slots = out_ref.shape[0]
    layers = keys_ref.shape[0]

    def body(slot, carry):
        for layer in range(layers):
            block = index_ref[layer, slot]
            pltpu.make_async_copy(
                keys_ref.at[layer, block], out_ref.at[slot, 2 * layer], sem
            ).start()
            pltpu.make_async_copy(
                values_ref.at[layer, block], out_ref.at[slot, 2 * layer + 1], sem
            ).start()
        return carry

    lax.fori_loop(0, slots, body, 0)
    pltpu.make_async_copy(out_ref, out_ref, sem).wait()


def pack(index, keys, values, after):
    layers, slots = index.shape
    return pl.pallas_call(
        pack_kernel,
        out_shape=jax.ShapeDtypeStruct((slots, 2 * layers) + keys.shape[2:], keys.dtype),
        in_specs=[
            pl.BlockSpec(memory_space=pltpu.SMEM),
            pl.BlockSpec(memory_space=pl.ANY),
            pl.BlockSpec(memory_space=pl.ANY),
            pl.BlockSpec(memory_space=pl.ANY),
        ],
        out_specs=pl.BlockSpec(memory_space=pl.ANY),
        scratch_shapes=[pltpu.SemaphoreType.DMA],
        compiler_params=pltpu.CompilerParams(vmem_limit_bytes=48 * MIB),
        cost_estimate=pl.CostEstimate(flops=0, bytes_accessed=16 * MIB, transcendentals=0),
        name="pack",
    )(index, keys, values, after)


def unpack_kernel(index_ref, got_ref, keys_ref, values_ref, sems):
    layers, count = index_ref.shape

    def body(entry, carry):
        for layer in range(layers):
            slot = index_ref[layer, entry]
            pltpu.make_async_copy(
                got_ref.at[slot, 2 * layer], keys_ref.at[layer, entry], sems.at[0]
            ).start()
            pltpu.make_async_copy(
                got_ref.at[slot, 2 * layer + 1], values_ref.at[layer, entry], sems.at[1]
            ).start()
        return carry

    lax.fori_loop(0, count, body, 0)
    pltpu.make_async_copy(keys_ref, keys_ref, sems.at[0]).wait()
    pltpu.make_async_copy(values_ref, values_ref, sems.at[1]).wait()


def unpack(index, got):
    layers, count = index.shape
    out = jax.ShapeDtypeStruct((layers, count) + got.shape[2:], got.dtype)
    return pl.pallas_call(
        unpack_kernel,
        out_shape=(out, out),
        in_specs=[pl.BlockSpec(memory_space=pltpu.SMEM), pl.BlockSpec(memory_space=pl.ANY)],
        out_specs=(pl.BlockSpec(memory_space=pltpu.VMEM), pl.BlockSpec(memory_space=pltpu.VMEM)),
        scratch_shapes=[pltpu.SemaphoreType.DMA((2,))],
        compiler_params=pltpu.CompilerParams(vmem_limit_bytes=48 * MIB),
        cost_estimate=pl.CostEstimate(flops=0, bytes_accessed=4 * MIB, transcendentals=0),
        name="unpack",
    )(index, got)


def logits(limit_ref, query_ref, key_ref, group, scale):
    raw = lax.dot_general(
        query_ref[0], key_ref[0], (((1,), (1,)), ((), ())), preferred_element_type=jnp.float32
    )
    start = pl.program_id(1) * TILE
    row = lax.broadcasted_iota(jnp.int32, raw.shape, 0) // group
    column = lax.broadcasted_iota(jnp.int32, raw.shape, 1) + start
    return jnp.where(column <= row + limit_ref[0], raw * scale, NEG)


def stats_kernel(group, scale, limit_ref, query_ref, key_ref, peak_ref, total_ref, peaks, totals):
    tile = pl.program_id(1)

    @pl.when(tile == 0)
    def _():
        peaks[...] = jnp.full_like(peaks, NEG)
        totals[...] = jnp.zeros_like(totals)

    score = logits(limit_ref, query_ref, key_ref, group, scale)
    rows, width = score.shape
    parts = [score[:, c : c + LANES] for c in range(0, width, LANES)]
    old = peaks[...]
    new = functools.reduce(jnp.maximum, parts, old)
    total = totals[...] * jnp.exp2(old - new)
    for part in parts:
        total = total + jnp.exp2(part - new)
    peaks[...] = new
    totals[...] = total

    @pl.when(tile == pl.num_programs(1) - 1)
    def _():
        peak = jnp.max(new, axis=1, keepdims=True)
        peak_ref[0] = peak
        total_ref[0] = jnp.sum(total * jnp.exp2(new - peak), axis=1, keepdims=True)


def local_stats(limit, query, keys, group, scale):
    layers, rows, head_dim = query.shape
    tiles = keys.shape[1] // TILE
    out = jax.ShapeDtypeStruct((layers, rows, 1), jnp.float32)
    spec = pl.BlockSpec((1, rows, 1), lambda l, t: (l, 0, 0))
    return pl.pallas_call(
        functools.partial(stats_kernel, group, scale),
        out_shape=(out, out),
        grid=(layers, tiles),
        in_specs=[
            pl.BlockSpec(memory_space=pltpu.SMEM),
            pl.BlockSpec((1, rows, head_dim), lambda l, t: (l, 0, 0)),
            pl.BlockSpec((1, TILE, head_dim), lambda l, t: (l, t, 0)),
        ],
        out_specs=(spec, spec),
        scratch_shapes=[pltpu.VMEM((rows, LANES), jnp.float32)] * 2,
        compiler_params=pltpu.CompilerParams(vmem_limit_bytes=32 * MIB),
        cost_estimate=pl.CostEstimate(
            flops=2 * layers * rows * keys.shape[1] * head_dim,
            bytes_accessed=keys.size * 2,
            transcendentals=layers * rows * keys.shape[1],
        ),
        name="stats",
    )(limit, query, keys)


def mass_kernel(
    group, scale, shard_len, total_len, limit_ref, query_ref, key_ref, edge_ref, peak_ref, factor_ref,
    mass_ref, edge_mass_ref,
):
    score = logits(limit_ref, query_ref, key_ref, group, scale)
    weight = jnp.exp2(score - peak_ref[0]) * factor_ref[0]
    mass_ref[0] = jnp.sum(weight, axis=0, keepdims=True)

    @pl.when(pl.program_id(1) == 0)
    def _():
        raw = lax.dot_general(
            query_ref[0],
            edge_ref[0],
            (((1,), (1,)), ((), ())),
            preferred_element_type=jnp.float32,
        )
        side = raw.shape[1] // 2
        row = lax.broadcasted_iota(jnp.int32, raw.shape, 0) // group
        column = lax.broadcasted_iota(jnp.int32, raw.shape, 1)
        column = jnp.where(column < side, column - side, column - side + shard_len)
        start = limit_ref[1]
        inside = (column + start >= 0) & (column + start < total_len)
        inside = inside & (column <= row + limit_ref[0])
        weight = jnp.exp2(jnp.where(inside, raw * scale, NEG) - peak_ref[0]) * factor_ref[0]
        edge_mass_ref[0] = jnp.sum(weight, axis=0, keepdims=True)


def local_mass(limit, query, keys, edges, peak, factor, group, scale, total_len):
    layers, rows, head_dim = query.shape
    shard_len = keys.shape[1]
    tiles = shard_len // TILE
    column = pl.BlockSpec((1, rows, 1), lambda l, t: (l, 0, 0))
    return pl.pallas_call(
        functools.partial(mass_kernel, group, scale, shard_len, total_len),
        out_shape=(
            jax.ShapeDtypeStruct((layers, 1, shard_len), jnp.float32),
            jax.ShapeDtypeStruct((layers, 1, edges.shape[1]), jnp.float32),
        ),
        grid=(layers, tiles),
        in_specs=[
            pl.BlockSpec(memory_space=pltpu.SMEM),
            pl.BlockSpec((1, rows, head_dim), lambda l, t: (l, 0, 0)),
            pl.BlockSpec((1, TILE, head_dim), lambda l, t: (l, t, 0)),
            pl.BlockSpec((1, edges.shape[1], head_dim), lambda l, t: (l, 0, 0)),
            column,
            column,
        ],
        out_specs=(
            pl.BlockSpec((1, 1, TILE), lambda l, t: (l, 0, t)),
            pl.BlockSpec((1, 1, edges.shape[1]), lambda l, t: (l, 0, 0)),
        ),
        compiler_params=pltpu.CompilerParams(vmem_limit_bytes=32 * MIB),
        cost_estimate=pl.CostEstimate(
            flops=2 * layers * rows * shard_len * head_dim,
            bytes_accessed=keys.size * 2,
            transcendentals=layers * rows * shard_len,
        ),
        name="mass",
    )(limit, query, keys, edges, peak, factor)


def broadcast_plan(width, fan):
    rounds = []
    step = width
    while step > 1:
        split = min(fan, step)
        step //= split
        rounds.append((split, step))
    return rounds


def spread(x, axis):
    width = lax.axis_size(axis)
    place = lax.axis_index(axis)
    span = width
    for split, step in broadcast_plan(width, 4):
        holders = [i for i in range(width) if (i + 1) % span == 0]
        held = (place + 1) % span == 0
        got = x
        moved = [
            lax.ppermute(x, axis, [(i, i - turn * step) for i in holders])
            for turn in range(1, split)
        ]
        merged = functools.reduce(jnp.add, moved)
        x = jnp.where(held, got, merged)
        span = step
    return x


def partners(axis, bit):
    return [(i, i ^ bit) for i in range(lax.axis_size(axis))]


def merge_stats(peak, total, axis):
    bit = 1
    both = jnp.stack([peak, total])
    while bit < lax.axis_size(axis):
        other = lax.ppermute(both, axis, partners(axis, bit))
        top = jnp.maximum(both[0], other[0])
        both = jnp.stack(
            [top, both[1] * jnp.exp2(both[0] - top) + other[1] * jnp.exp2(other[0] - top)]
        )
        bit *= 2
    return both[0], both[1]


def total_over(x, axis):
    bit = 1
    while bit < lax.axis_size(axis):
        x = x + lax.ppermute(x, axis, partners(axis, bit))
        bit *= 2
    return x


def per_device(keys, values, queries, keep_blocks, block_owner):
    width = lax.axis_size("ctx")
    position = lax.axis_index("ctx")
    layers, shard_len, heads_here, head_dim = keys.shape
    window = queries.shape[1]
    group = queries.shape[2] // heads_here
    total_len = shard_len * width
    rows = window * group
    blocks_here = shard_len // BLOCK
    keep_count = keep_blocks.shape[2]
    keep_share = keep_count // width
    capacity = (blocks_here + width - 1) // width
    keys = keys.reshape(layers, shard_len, head_dim)
    values = values.reshape(layers, shard_len, head_dim)
    kept = keep_blocks[:, 0]
    owner = block_owner[:, 0]
    source = kept // blocks_here
    entry = jnp.arange(keep_count, dtype=jnp.int32)
    earlier = entry[None, :] < entry[:, None]
    same_owner = owner[:, :, None] == owner[:, None, :]
    same_source = source[:, :, None] == source[:, None, :]
    owner_rank = jnp.sum(same_owner & earlier, axis=-1)
    pair_rank = jnp.sum(same_owner & same_source & earlier, axis=-1)
    slot = owner * capacity + pair_rank
    send_hit = (source == position)[..., None] & (
        slot[..., None] == jnp.arange(width * capacity, dtype=jnp.int32)
    )
    send_index = jnp.sum(jnp.where(send_hit, (kept % blocks_here)[..., None], 0), axis=1)
    recv_hit = (owner == position)[..., None] & (
        owner_rank[..., None] == jnp.arange(keep_share, dtype=jnp.int32)
    )
    recv_index = jnp.sum(jnp.where(recv_hit, (source * capacity + pair_rank)[..., None], 0), axis=1)

    side = 8
    half = (POOL - 1) // 2
    forward = [(i, i + 1) for i in range(width - 1)]
    backward = [(i + 1, i) for i in range(width - 1)]
    low = lax.ppermute(keys[:, shard_len - side :], "ctx", forward)
    high = lax.ppermute(keys[:, :side], "ctx", backward)
    edges = jnp.concatenate([low, high], axis=1)
    windowed = spread(queries, "ctx").reshape(layers, rows, head_dim)
    start = position * shard_len
    limit = jnp.stack([total_len - window - start, start])
    scale = head_dim**-0.5 * math.log2(math.e)
    peak, total = local_stats(limit, windowed, keys, group, scale)
    peak, total = merge_stats(peak.reshape(layers, rows), total.reshape(layers, rows), "ctx")

    blocked = (layers, blocks_here, BLOCK, head_dim)
    parcels = pack(send_index, keys.reshape(blocked), values.reshape(blocked), total)
    got = lax.all_to_all(parcels, "ctx", split_axis=0, concat_axis=0, tiled=True)

    factor = (total_len / rows) / total
    mass, edge_mass = local_mass(
        limit, windowed, keys, edges, peak[..., None], factor[..., None], group, scale, total_len
    )
    padded = jnp.concatenate(
        [edge_mass[:, 0, side - half : side], mass[:, 0], edge_mass[:, 0, side : side + half]],
        axis=1,
    )
    pooled = padded[:, 0:shard_len]
    for shift in range(1, POOL):
        pooled = pooled + padded[:, shift : shift + shard_len]
    pooled = pooled / POOL
    shared = total_over(pooled, "head") / KVH
    block_mass = jnp.sum(pooled.reshape(layers, blocks_here, BLOCK), axis=2).astype(jnp.bfloat16)
    sent_mass = jnp.take_along_axis(block_mass, send_index, axis=1)
    got_mass = lax.all_to_all(sent_mass, "ctx", split_axis=1, concat_axis=1, tiled=True)
    kept_mass = jnp.take_along_axis(got_mass, recv_index, axis=1)

    compact_keys, compact_values = unpack(recv_index, got)
    share = (layers, heads_here, keep_share * BLOCK, head_dim)
    return (
        pooled[:, None],
        shared,
        compact_keys.reshape(share),
        compact_values.reshape(share),
        kept_mass[:, None],
    )


def solution(mesh):
    in_specs = (
        P(None, "ctx", "head", None),
        P(None, "ctx", "head", None),
        P(None, "ctx", "head", None),
        P(None, "head", None),
        P(None, "head", None),
    )
    out_specs = (
        P(None, "head", "ctx"),
        P(None, "ctx"),
        P(None, "head", "ctx", None),
        P(None, "head", "ctx", None),
        P(None, "head", "ctx"),
    )
    return jax.shard_map(
        per_device, mesh=mesh, in_specs=in_specs, out_specs=out_specs, check_vma=False
    )
```

time: 575 us -> 433 us (0.75)
  blocking collectives: 219 us -> 0 us
  Pallas kernels: 0 us -> 157 us
  other arithmetic: 47.3 us -> 5.89 us
  starting transfers between devices: 31.2 us -> 64.2 us
  local copies, waits for them, and re-layouts: 38.2 us -> 13.1 us
  waiting for transfers between devices: 207 us -> 188 us
  matrix products: 17.6 us -> 0 us
  between operations: 14.3 us -> 1.06 us
    psum x2 -> x0, waiting for transfers between devices: 197 us -> none  [the longest x1 129 us: spread(): return lax.psum(jnp.where(mine, x, jnp.zeros_like(x)), axis)]
    all_to_all x2, waiting for transfers between devices: 3.49 us -> 164 us  [the longest x1 164 us: per_device(): lax.all_to_all(parcels, 'ctx', split_axis=0, concat_axis=0, tiled=True)]
    pallas_call x0 -> x4, Pallas kernels: none -> 157 us  [the longest x1 129 us: pack(): pl.pallas_call(pack_kernel, out_shape=jax.ShapeDtypeStruct((slots, 2 * la...]
    all_to_all x1 -> x0, blocking collectives: 88 us -> none  [per_device(): lax.all_to_all(key_parcels, 'ctx', split_axis=2, concat_axis=2, tiled=True)]
    psum x1 -> x0, blocking collectives: 68.3 us -> none  [per_device(): lax.psum(jnp.stack([jnp.sum(jnp.exp(scores(l, g) - peaks[index][:, None])...]
    pmax x1 -> x0, blocking collectives: 63 us -> none  [per_device(): lax.pmax(jnp.stack([jnp.max(scores(l, g), axis=1) for l, g in pairs]), 'c...]
    ppermute x2 -> x17, starting transfers between devices: 9.14 us -> 42 us  [the longest x5 21.3 us: merge_stats(): other = lax.ppermute(both, axis, partners(axis, bit))]
    reduce_sum x6 -> x2, other arithmetic: 31.5 us -> 0.24 us  [the longest x1 0.15 us: per_device(): jnp.sum(jnp.where(send_hit, (kept % blocks_here)[..., None], 0), axis=1)]
  transfers between devices with their start and end apart: 6 -> 19, of which waited for: 4 -> 10; matrix products, arithmetic and copies ran while one was open for 6% -> 2% of each run, Pallas kernels for 0% -> 33%
where the time goes in v1:
time: 433 us; the launch traced here: 430 us
  waiting for transfers between devices  188 us (43%)
  Pallas kernels  157 us (36%)
  starting transfers between devices  64.2 us (15%)
  local copies, waits for them, and re-layouts  13.1 us (3%)
  other arithmetic  5.89 us (1%)
    all_to_all x1, waiting for transfers between devices, per_device(): lax.all_to_all(parcels, 'ctx', split_axis=0, concat_axis=0, tiled=True)  164 us
    pallas_call x1, Pallas kernels, pack(): pl.pallas_call(pack_kernel, out_shape=jax.ShapeDtypeStruct((slots, 2 * la...  129 us
    ppermute x5, starting transfers between devices, merge_stats(): other = lax.ppermute(both, axis, partners(axis, bit))  21.3 us
    pallas_call x1, Pallas kernels, local_stats(): pl.pallas_call(functools.partial(stats_kernel, group, scale), out_shape=(...  12.7 us
    all_to_all x1, starting transfers between devices, per_device(): lax.all_to_all(sent_mass, 'ctx', split_axis=1, concat_axis=1, tiled=True)  12.4 us
    pallas_call x1, Pallas kernels, local_mass(): pl.pallas_call(functools.partial(mass_kernel, group, scale, shard_len, to...  12.3 us
    ppermute x7, waiting for transfers between devices, spread(): lax.ppermute(x, axis, [(i, i - turn * step) for i in holders])  11.3 us
    all_to_all x1, starting transfers between devices, per_device(): lax.all_to_all(parcels, 'ctx', split_axis=0, concat_axis=0, tiled=True)  9.85 us
  transfers between devices with their start and end apart: 19, of which 10 were waited for; matrix products, arithmetic and copies ran while one was open for 2% of the time, Pallas kernels for 33%

profile of v1, /device:TPU:2, one launch (start us, length us, event | category | flops | bytes accessed | tf_op | source)
XLA Modules:
  0.0 429.8 jit_solution(13151566953590548924)
XLA Ops:
  0.6 0.7 collective-permute-start.1
  1.3 0.7 collective-permute-start
  2.0 0.7 collective-permute-start.2
  2.7 0.7 fusion.84
  3.4 3.8 collective-permute-start.7
  7.2 6.4 %collective-permute-start.8 = (bf16[2,8,128]{2,1,0:T(8,128)(2,1)S(1)}, bf16[2,8,128]{2,1,0:T(8,128)(2,1)S(1)}, u32[]{:S(2)}, u32[]{:S(2)}) collective-permute-start(bf16[2,8,128]{2,1,0:T(8,128)(2,1)S(1)} %get-tuple-element.50), channel_id=1, source_target_pairs={{8,0},{16,8},{24,16},{32,24},{40,32},{48,40},{56,48},{64,56},{72,6... | collective-permute-start | bytes 12296 | tf_op jit(solution)/shard_map/ppermute | solution.py:305
  13.7 0.7 and_select_fusion.1
  14.4 0.7 broadcast_compare_fusion.1
  15.2 0.7 collective-permute-start.5
  15.9 0.7 collective-permute-start.4
  16.6 0.7 collective-permute-start.3
  17.3 0.1 iota_compare_fusion
  17.4 0.7 copy_bitcast_fusion.1
  18.2 1.3 collective-permute-start.6
  19.5 1.4 convert_reduce_fusion.1
  20.9 11.3 %collective-permute-done.6 = bf16[2,64,8,128]{3,2,1,0:T(8,128)(2,1)S(1)} collective-permute-done((bf16[2,64,8,128]{3,2,1,0:T(8,128)(2,1)S(1)}, bf16[2,64,8,128]{3,2,1,0:T(8,128)(2,1)S(1)}, u32[]{:S(2)}, u32[]{:S(2)}) %collective-permute-start.6) | collective-permute-done | bytes 262176 | tf_op jit(solution)/shard_map/ppermute | solution.py:233
  32.2 2.2 copy-done
  34.4 12.7 %stats.1 = (f32[2,512,1]{2,1,0:T(8,128)S(1)}, f32[2,512,1]{2,1,0:T(8,128)S(1)}) custom-call(s32[2]{0:T(128)S(1)} %pad_add_fusion.limit_ref, bf16[2,512,128]{2,1,0:T(8,128)(2,1)S(1)} %select_bitcast_fusion.query_ref, bf16[2,8192,128]{2,1,0:T(8,128)(2,1)S(1)} %bitcast.306), custom_call_target="tpu_custom_call" | custom-call | flops 2147483648 | bytes 4194304 | tf_op jit(solution)/shard_map/stats/pallas_call | solution.py:132
  47.1 0.2 reduce
  47.3 0.2 reduce.1
  47.6 0.1 collective-permute-start.9
  47.7 3.6 collective-permute-done.9
  51.3 6.6 %collective-permute-start.10 = (f32[2,2,512]{2,1,0:T(2,128)S(1)}, f32[2,2,512]{2,1,0:T(2,128)S(1)}, u32[]{:S(2)}, u32[]{:S(2)}) collective-permute-start(f32[2,2,512]{2,1,0:T(2,128)S(1)} %pad_maximum_fusion.4), channel_id=1, source_target_pairs={{0,16},{8,24},{16,0},{24,8},{32,48},{40,56},{48,32},{56,40},{64,80... | collective-permute-start | bytes 24584 | tf_op jit(solution)/shard_map/ppermute | solution.py:250
  58.0 1.6 collective-permute-done.10
  59.6 7.4 %collective-permute-start.11 = (f32[2,2,512]{2,1,0:T(2,128)S(1)}, f32[2,2,512]{2,1,0:T(2,128)S(1)}, u32[]{:S(2)}, u32[]{:S(2)}) collective-permute-start(f32[2,2,512]{2,1,0:T(2,128)S(1)} %pad_maximum_fusion.5), channel_id=1, source_target_pairs={{0,32},{8,40},{16,48},{24,56},{32,0},{40,8},{48,16},{56,24},{64,96... | collective-permute-start | bytes 24584 | tf_op jit(solution)/shard_map/ppermute | solution.py:250
  67.1 0.2 select_reduce_fusion.index_ref
  67.2 1.5 collective-permute-done.11
  68.7 2.5 collective-permute-start.12
  71.3 0.1 reduce_sum.58
  71.4 0.1 reshape.229
  71.4 1.4 collective-permute-done.12
  72.9 4.6 %collective-permute-start.13 = (f32[2,2,512]{2,1,0:T(2,128)S(1)}, f32[2,2,512]{2,1,0:T(2,128)S(1)}, u32[]{:S(2)}, u32[]{:S(2)}) collective-permute-start(f32[2,2,512]{2,1,0:T(2,128)S(1)} %pad_maximum_fusion.7), channel_id=1, source_target_pairs={{0,128},{8,136},{16,144},{24,152},{32,160},{40,168},{48,176},{56,1... | collective-permute-start | bytes 24584 | tf_op jit(solution)/shard_map/ppermute | solution.py:250
  77.5 0.2 copy.36
  77.7 0.2 copy.38
  77.9 1.2 collective-permute-done.13
  79.2 0.2 copy.40.factor_ref
  79.4 0.2 copy.39.peak_ref
  79.7 2.2 copy-done.1
  81.9 12.3 %mass.1 = (f32[2,1,8192]{2,1,0:T(1,128)S(1)}, f32[2,1,16]{2,1,0:T(1,128)S(1)}) custom-call(s32[2]{0:T(128)S(1)} %pad_add_fusion.limit_ref, bf16[2,512,128]{2,1,0:T(8,128)(2,1)S(1)} %select_bitcast_fusion.query_ref, bf16[2,8192,128]{2,1,0:T(8,128)(2,1)S(1)} %bitcast.307, bf16[2,16,128]{2,1,0:T(8,128)(2,1)S(1)} %pad_maximum_fusion.2.edge_ref, ...), custom_call_target="tpu_custom_call" | custom-call | flops 2147483648 | bytes 4194304 | tf_op jit(solution)/shard_map/mass/pallas_call | solution.py:185
  94.3 0.5 fusion.13
  94.8 0.1 bitcast_reduce_fusion
  94.9 1.5 gather_fusion
  96.4 0.1 gather.13
  96.6 0.6 copy.41
  97.2 12.4 %all-to-all-start.1 = ((bf16[2,32,2]{2,0,1:T(2,128)(2,1)}), bf16[2,32,2]{2,0,1:T(2,128)(2,1)S(1)}, u32[]{:S(2)}, u32[]{:S(2)}) async-start(bf16[2,32,2]{2,0,1:T(2,128)(2,1)} %copy.41), calls=%async_computation.1 | async-start | bytes 32768 | tf_op jit(solution)/shard_map/all_to_all | solution.py:333
  109.6 2.2 copy-done.2
  111.8 128.7 %pack.1 = bf16[64,4,128,128]{3,2,1,0:T(8,128)(2,1)} custom-call(s32[2,64]{1,0:T(2,128)S(1)} %select_reduce_fusion.index_ref, bf16[2,64,128,128]{3,2,1,0:T(8,128)(2,1)S(1)} %bitcast.308, bf16[2,64,128,128]{3,2,1,0:T(8,128)(2,1)} %bitcast.309, f32[2,512]{1,0:T(2,128)S(1)} %fusion.17.after_ref), custom_call_target="tpu_custom_call" | custom-call | bytes 16777216 | tf_op jit(solution)/shard_map/pack/pallas_call | solution.py:40
  240.5 9.9 %all-to-all-start = ((bf16[64,4,128,128]{3,2,1,0:T(8,128)(2,1)}), bf16[64,4,128,128]{3,2,1,0:T(8,128)(2,1)}, u32[]{:S(2)}, u32[]{:S(2)}) async-start(bf16[64,4,128,128]{3,2,1,0:T(8,128)(2,1)} %pack.1), calls=%async_computation | async-start | bytes 16777216 | tf_op jit(solution)/shard_map/all_to_all | solution.py:316
  250.4 0.1 collective-permute-start.14
  250.5 0.1 select_reduce_fusion.1.index_ref
  250.7 1.1 collective-permute-done.14
  251.8 1.7 collective-permute-start.15
  253.5 0.1 reshape.235
  253.6 0.7 copy.43
  254.3 0.1 all_to_all.11
  254.4 0.7 gather_fusion.1
  255.1 0.1 gather.15
  255.2 0.9 collective-permute-done.15
  256.2 3.3 collective-permute-start.16
  259.5 0.5 and_select_fusion.4
  260.0 2.1 collective-permute-done.16
  262.1 0.7 add_multiply_fusion
  262.7 163.7 %all-to-all-done.got_ref = bf16[64,4,128,128]{3,2,1,0:T(8,128)(2,1)} async-done(((bf16[64,4,128,128]{3,2,1,0:T(8,128)(2,1)}), bf16[64,4,128,128]{3,2,1,0:T(8,128)(2,1)}, u32[]{:S(2)}, u32[]{:S(2)}) %all-to-all-start) | async-done | bytes 8388640 | tf_op jit(solution)/shard_map/all_to_all | solution.py:316
  426.4 3.4 unpack.1
  (43 shorter events, 0.7 us)
Async XLA Ops:
  0.6 14.5 %collective-permute-start.1 = (bf16[2,64,8,128]{3,2,1,0:T(8,128)(2,1)}, bf16[2,64,8,128]{3,2,1,0:T(8,128)(2,1)S(1)}, u32[]{:S(2)}, u32[]{:S(2)}) collective-permute-start(bf16[2,64,8,128]{3,2,1,0:T(8,128)(2,1)} %param.7), channel_id=1, source_target_pairs={{248,120},{249,121},{250,122},{251,123},{252,124},{253,125},{254,1... | collective-permute-start | bytes 786440 | tf_op jit(solution)/shard_map/ppermute | solution.py:233
  1.3 13.8 %collective-permute-start = (bf16[2,64,8,128]{3,2,1,0:T(8,128)(2,1)}, bf16[2,64,8,128]{3,2,1,0:T(8,128)(2,1)S(1)}, u32[]{:S(2)}, u32[]{:S(2)}) collective-permute-start(bf16[2,64,8,128]{3,2,1,0:T(8,128)(2,1)} %param.7), channel_id=1, source_target_pairs={{248,184},{249,185},{250,186},{251,187},{252,188},{253,189},{254,1... | collective-permute-start | bytes 786440 | tf_op jit(solution)/shard_map/ppermute | solution.py:233
  2.0 13.1 %collective-permute-start.2 = (bf16[2,64,8,128]{3,2,1,0:T(8,128)(2,1)}, bf16[2,64,8,128]{3,2,1,0:T(8,128)(2,1)S(1)}, u32[]{:S(2)}, u32[]{:S(2)}) collective-permute-start(bf16[2,64,8,128]{3,2,1,0:T(8,128)(2,1)} %param.7), channel_id=1, source_target_pairs={{248,56},{249,57},{250,58},{251,59},{252,60},{253,61},{254,62},{25... | collective-permute-start | bytes 786440 | tf_op jit(solution)/shard_map/ppermute | solution.py:233
  3.4 74.1 %collective-permute-start.7 = (bf16[2,8,128]{2,1,0:T(8,128)(2,1)S(1)}, bf16[2,8,128]{2,1,0:T(8,128)(2,1)S(1)}, u32[]{:S(2)}, u32[]{:S(2)}) collective-permute-start(bf16[2,8,128]{2,1,0:T(8,128)(2,1)S(1)} %get-tuple-element.49), channel_id=1, source_target_pairs={{0,8},{8,16},{16,24},{24,32},{32,40},{40,48},{48,56},{56,64},{64,7... | collective-permute-start | bytes 12296 | tf_op jit(solution)/shard_map/ppermute | solution.py:304
  7.2 70.3 %collective-permute-start.8 = (bf16[2,8,128]{2,1,0:T(8,128)(2,1)S(1)}, bf16[2,8,128]{2,1,0:T(8,128)(2,1)S(1)}, u32[]{:S(2)}, u32[]{:S(2)}) collective-permute-start(bf16[2,8,128]{2,1,0:T(8,128)(2,1)S(1)} %get-tuple-element.50), channel_id=1, source_target_pairs={{8,0},{16,8},{24,16},{32,24},{40,32},{48,40},{56,48},{64,56},{72,6... | collective-permute-start | bytes 12296 | tf_op jit(solution)/shard_map/ppermute | solution.py:305
  15.2 2.9 collective-permute-start.5
  15.9 2.2 collective-permute-start.4
  16.6 1.5 collective-permute-start.3
  18.2 14.0 %collective-permute-start.6 = (bf16[2,64,8,128]{3,2,1,0:T(8,128)(2,1)S(1)}, bf16[2,64,8,128]{3,2,1,0:T(8,128)(2,1)S(1)}, u32[]{:S(2)}, u32[]{:S(2)}) collective-permute-start(bf16[2,64,8,128]{3,2,1,0:T(8,128)(2,1)S(1)} %add_select_fusion), channel_id=1, source_target_pairs={{8,0},{24,16},{40,32},{56,48},{72,64},{88,80},{104,96},{120,112},{... | collective-permute-start | bytes 786440 | tf_op jit(solution)/shard_map/ppermute | solution.py:233
  32.2 2.2 copy-start
  34.4 13.3 %copy-start.4 = (s32[2,1,512]{2,1,0:T(1,128)S(1)}, s32[2,1,512]{2,1,0:T(1,128)}, u32[]{:S(2)}) copy-start(s32[2,1,512]{2,1,0:T(1,128)} %param.9) | copy-start | bytes 12292
  34.4 23.6 %copy-start.3 = (s32[2,1,512]{2,1,0:T(1,128)S(1)}, s32[2,1,512]{2,1,0:T(1,128)}, u32[]{:S(2)}) copy-start(s32[2,1,512]{2,1,0:T(1,128)} %param.8) | copy-start | bytes 12292
  47.6 3.7 collective-permute-start.9
  51.3 8.3 %collective-permute-start.10 = (f32[2,2,512]{2,1,0:T(2,128)S(1)}, f32[2,2,512]{2,1,0:T(2,128)S(1)}, u32[]{:S(2)}, u32[]{:S(2)}) collective-permute-start(f32[2,2,512]{2,1,0:T(2,128)S(1)} %pad_maximum_fusion.4), channel_id=1, source_target_pairs={{0,16},{8,24},{16,0},{24,8},{32,48},{40,56},{48,32},{56,40},{64,80... | collective-permute-start | bytes 24584 | tf_op jit(solution)/shard_map/ppermute | solution.py:250
  59.6 9.1 %collective-permute-start.11 = (f32[2,2,512]{2,1,0:T(2,128)S(1)}, f32[2,2,512]{2,1,0:T(2,128)S(1)}, u32[]{:S(2)}, u32[]{:S(2)}) collective-permute-start(f32[2,2,512]{2,1,0:T(2,128)S(1)} %pad_maximum_fusion.5), channel_id=1, source_target_pairs={{0,32},{8,40},{16,48},{24,56},{32,0},{40,8},{48,16},{56,24},{64,96... | collective-permute-start | bytes 24584 | tf_op jit(solution)/shard_map/ppermute | solution.py:250
  68.7 4.1 collective-permute-start.12
  72.9 6.2 %collective-permute-start.13 = (f32[2,2,512]{2,1,0:T(2,128)S(1)}, f32[2,2,512]{2,1,0:T(2,128)S(1)}, u32[]{:S(2)}, u32[]{:S(2)}) collective-permute-start(f32[2,2,512]{2,1,0:T(2,128)S(1)} %pad_maximum_fusion.7), channel_id=1, source_target_pairs={{0,128},{8,136},{16,144},{24,152},{32,160},{40,168},{48,176},{56,1... | collective-permute-start | bytes 24584 | tf_op jit(solution)/shard_map/ppermute | solution.py:250
  79.7 2.2 copy-start.1
  97.2 143.3 %all-to-all-start.1 = ((bf16[2,32,2]{2,0,1:T(2,128)(2,1)}), bf16[2,32,2]{2,0,1:T(2,128)(2,1)S(1)}, u32[]{:S(2)}, u32[]{:S(2)}) async-start(bf16[2,32,2]{2,0,1:T(2,128)(2,1)} %copy.41), calls=%async_computation.1 | async-start | bytes 32768 | tf_op jit(solution)/shard_map/all_to_all | solution.py:333
  109.6 2.2 copy-start.2
  240.5 185.9 %all-to-all-start = ((bf16[64,4,128,128]{3,2,1,0:T(8,128)(2,1)}), bf16[64,4,128,128]{3,2,1,0:T(8,128)(2,1)}, u32[]{:S(2)}, u32[]{:S(2)}) async-start(bf16[64,4,128,128]{3,2,1,0:T(8,128)(2,1)} %pack.1), calls=%async_computation | async-start | bytes 16777216 | tf_op jit(solution)/shard_map/all_to_all | solution.py:316
  250.4 1.3 collective-permute-start.14
  251.8 4.4 %collective-permute-start.15 = (f32[2,8192]{1,0:T(2,128)S(1)}, f32[2,8192]{1,0:T(2,128)S(1)}, u32[]{:S(2)}, u32[]{:S(2)}) collective-permute-start(f32[2,8192]{1,0:T(2,128)S(1)} %add.210), channel_id=1, source_target_pairs={{0,2},{1,3},{2,0},{3,1},{4,6},{5,7},{6,4},{7,5},{8,10},{9,11},{10,... | collective-permute-start | bytes 196616 | tf_op jit(solution)/shard_map/ppermute | solution.py:262
  256.2 5.9 %collective-permute-start.16 = (f32[2,8192]{1,0:T(2,128)S(1)}, f32[2,8192]{1,0:T(2,128)S(1)}, u32[]{:S(2)}, u32[]{:S(2)}) collective-permute-start(f32[2,8192]{1,0:T(2,128)S(1)} %add.211), channel_id=1, source_target_pairs={{0,4},{1,5},{2,6},{3,7},{4,0},{5,1},{6,2},{7,3},{8,12},{9,13},{10,... | collective-permute-start | bytes 196616 | tf_op jit(solution)/shard_map/ppermute | solution.py:262

commit v2 on v1

--- a/solution.py
+++ b/solution.py
@@ -16,42 +16,52 @@
 MIB = 1 << 20
 
 
-def pack_kernel(index_ref, keys_ref, values_ref, after_ref, out_ref, sem):
-    slots = out_ref.shape[0]
-    layers = keys_ref.shape[0]
-
-    def body(slot, carry):
-        for layer in range(layers):
-            block = index_ref[layer, slot]
-            pltpu.make_async_copy(
-                keys_ref.at[layer, block], out_ref.at[slot, 2 * layer], sem
-            ).start()
-            pltpu.make_async_copy(
-                values_ref.at[layer, block], out_ref.at[slot, 2 * layer + 1], sem
-            ).start()
-        return carry
-
-    lax.fori_loop(0, slots, body, 0)
-    pltpu.make_async_copy(out_ref, out_ref, sem).wait()
-
-
-def pack(index, keys, values, after):
+def pack_kernel(first, parts, index_ref, keys_ref, values_ref, *rest):
+    out_ref = rest[-1]
+    step = first + pl.program_id(0)
+    layer, part = step // parts, step % parts
+    share = out_ref.shape[0]
+    for slot in range(share):
+        block = index_ref[layer, part * share + slot]
+        out_ref[slot, 0] = keys_ref[0, block]
+        out_ref[slot, 1] = values_ref[0, block]
+
+
+def pack(index, keys, values, first, count, after, parcels=None):
     layers, slots = index.shape
+    parts = 2
+    whole = pl.BlockSpec((1,) + keys.shape[1:], lambda i: ((first + i) // parts, 0, 0, 0))
+    others = [after] if parcels is None else [after, parcels]
     return pl.pallas_call(
-        pack_kernel,
+        functools.partial(pack_kernel, first, parts),
         out_shape=jax.ShapeDtypeStruct((slots, 2 * layers) + keys.shape[2:], keys.dtype),
-        in_specs=[
-            pl.BlockSpec(memory_space=pltpu.SMEM),
-            pl.BlockSpec(memory_space=pl.ANY),
-            pl.BlockSpec(memory_space=pl.ANY),
-            pl.BlockSpec(memory_space=pl.ANY),
-        ],
+        grid=(count,),
+        in_specs=[pl.BlockSpec(memory_space=pltpu.SMEM), whole, whole]
+        + [pl.BlockSpec(memory_space=pl.ANY)] * len(others),
+        out_specs=pl.BlockSpec(
+            (slots // parts, 2) + keys.shape[2:],
+            lambda i: ((first + i) % parts, (first + i) // parts, 0, 0),
+        ),
+        input_output_aliases={} if parcels is None else {4: 0},
+        compiler_params=pltpu.CompilerParams(vmem_limit_bytes=60 * MIB),
+        cost_estimate=pl.CostEstimate(flops=0, bytes_accessed=8 * MIB, transcendentals=0),
+        name="pack",
+    )(index, keys, values, *others)
+
+
+def gate_kernel(*refs):
+    pass
+
+
+def gate(array, *after):
+    return pl.pallas_call(
+        gate_kernel,
+        out_shape=jax.ShapeDtypeStruct(array.shape, array.dtype),
+        in_specs=[pl.BlockSpec(memory_space=pl.ANY)] * (1 + len(after)),
         out_specs=pl.BlockSpec(memory_space=pl.ANY),
-        scratch_shapes=[pltpu.SemaphoreType.DMA],
-        compiler_params=pltpu.CompilerParams(vmem_limit_bytes=48 * MIB),
-        cost_estimate=pl.CostEstimate(flops=0, bytes_accessed=16 * MIB, transcendentals=0),
-        name="pack",
-    )(index, keys, values, after)
+        input_output_aliases={0: 0},
+        name="gate",
+    )(array, *after)
 
 
 def unpack_kernel(index_ref, got_ref, keys_ref, values_ref, sems):
@@ -82,7 +92,7 @@
         in_specs=[pl.BlockSpec(memory_space=pltpu.SMEM), pl.BlockSpec(memory_space=pl.ANY)],
         out_specs=(pl.BlockSpec(memory_space=pltpu.VMEM), pl.BlockSpec(memory_space=pltpu.VMEM)),
         scratch_shapes=[pltpu.SemaphoreType.DMA((2,))],
-        compiler_params=pltpu.CompilerParams(vmem_limit_bytes=48 * MIB),
+        compiler_params=pltpu.CompilerParams(vmem_limit_bytes=60 * MIB),
         cost_estimate=pl.CostEstimate(flops=0, bytes_accessed=4 * MIB, transcendentals=0),
         name="unpack",
     )(index, got)
@@ -140,7 +150,7 @@
         ],
         out_specs=(spec, spec),
         scratch_shapes=[pltpu.VMEM((rows, LANES), jnp.float32)] * 2,
-        compiler_params=pltpu.CompilerParams(vmem_limit_bytes=32 * MIB),
+        compiler_params=pltpu.CompilerParams(vmem_limit_bytes=60 * MIB),
         cost_estimate=pl.CostEstimate(
             flops=2 * layers * rows * keys.shape[1] * head_dim,
             bytes_accessed=keys.size * 2,
@@ -201,7 +211,7 @@
             pl.BlockSpec((1, 1, TILE), lambda l, t: (l, 0, t)),
             pl.BlockSpec((1, 1, edges.shape[1]), lambda l, t: (l, 0, 0)),
         ),
-        compiler_params=pltpu.CompilerParams(vmem_limit_bytes=32 * MIB),
+        compiler_params=pltpu.CompilerParams(vmem_limit_bytes=60 * MIB),
         cost_estimate=pl.CostEstimate(
             flops=2 * layers * rows * shard_len * head_dim,
             bytes_accessed=keys.size * 2,
@@ -211,49 +221,69 @@
     )(limit, query, keys, edges, peak, factor)
 
 
-def broadcast_plan(width, fan):
-    rounds = []
-    step = width
-    while step > 1:
-        split = min(fan, step)
-        step //= split
-        rounds.append((split, step))
-    return rounds
-
-
-def spread(x, axis):
+def grid_of(axis):
     width = lax.axis_size(axis)
+    deep = 8 if width % 8 == 0 else width
+    return width // deep, deep
+
+
+def spread(x, axis, works):
+    wide, deep = grid_of(axis)
     place = lax.axis_index(axis)
-    span = width
-    for split, step in broadcast_plan(width, 4):
-        holders = [i for i in range(width) if (i + 1) % span == 0]
-        held = (place + 1) % span == 0
-        got = x
+    across, along = place // deep, place % deep
+    last = wide * deep - 1
+    pieces = x.reshape((wide, -1) + x.shape[2:])
+    moved = [
+        lax.ppermute(pieces[k], axis, [(last, k * deep + deep - 1)]) for k in range(wide - 1)
+    ]
+    piece = jnp.where(place == last, pieces[wide - 1], functools.reduce(jnp.add, moved))
+    held, result = [deep - 1], None
+    for work, steps in zip(works, (range(2, deep, 2), (1,))):
         moved = [
-            lax.ppermute(x, axis, [(i, i - turn * step) for i in holders])
-            for turn in range(1, split)
+            lax.ppermute(
+                piece,
+                axis,
+                [(k * deep + z, k * deep + (z + dz) % deep) for k in range(wide) for z in held],
+            )
+            for dz in steps
         ]
-        merged = functools.reduce(jnp.add, moved)
-        x = jnp.where(held, got, merged)
-        span = step
-    return x
+        result = work(piece, result)
+        mine = functools.reduce(jnp.logical_or, [along == z for z in held])
+        piece = jnp.where(mine, piece, functools.reduce(jnp.add, moved))
+        piece = gate(piece, result)
+        held = held + [(z + dz) % deep for z in held for dz in steps]
+    moved = [piece] + [
+        lax.ppermute(
+            piece,
+            axis,
+            [(k * deep + z, (k + dx) % wide * deep + z) for k in range(wide) for z in range(deep)],
+        )
+        for dx in range(1, wide)
+    ]
+    whole = [lax.select_n((across - k) % wide, *moved) for k in range(wide)]
+    return jnp.stack(whole).reshape(x.shape), result, moved[1:]
 
 
 def partners(axis, bit):
     return [(i, i ^ bit) for i in range(lax.axis_size(axis))]
 
 
-def merge_stats(peak, total, axis):
-    bit = 1
-    both = jnp.stack([peak, total])
-    while bit < lax.axis_size(axis):
-        other = lax.ppermute(both, axis, partners(axis, bit))
-        top = jnp.maximum(both[0], other[0])
-        both = jnp.stack(
-            [top, both[1] * jnp.exp2(both[0] - top) + other[1] * jnp.exp2(other[0] - top)]
-        )
-        bit *= 2
-    return both[0], both[1]
+def merge_stats(peak, total, ends, axis):
+    layers, rows = peak.shape
+    ends = ends.astype(jnp.float32).reshape(2, -1, rows)
+    both = [peak, total, ends[0], ends[1]]
+    used = sum(part.shape[0] for part in both)
+    both = jnp.concatenate(both + [jnp.zeros((16 - used, rows), jnp.float32)], axis=0)
+    every = lax.all_gather(both, axis, axis=0, tiled=False)
+    peaks, totals = every[:, :layers], every[:, layers : 2 * layers]
+    top = jnp.max(peaks, axis=0)
+    total = jnp.sum(totals * jnp.exp2(peaks - top), axis=0)
+    place, width = lax.axis_index(axis), lax.axis_size(axis)
+    count = ends.shape[1]
+    below = lax.dynamic_index_in_dim(every, jnp.maximum(place - 1, 0), 0, keepdims=False)
+    above = lax.dynamic_index_in_dim(every, jnp.minimum(place + 1, width - 1), 0, keepdims=False)
+    first = 2 * layers
+    return top, total, below[first : first + count], above[first + count : first + 2 * count]
 
 
 def total_over(x, axis):
@@ -275,11 +305,37 @@
     blocks_here = shard_len // BLOCK
     keep_count = keep_blocks.shape[2]
     keep_share = keep_count // width
-    capacity = (blocks_here + width - 1) // width
+    capacity = 2
     keys = keys.reshape(layers, shard_len, head_dim)
     values = values.reshape(layers, shard_len, head_dim)
-    kept = keep_blocks[:, 0]
-    owner = block_owner[:, 0]
+    kept, owner = keep_blocks[:, 0], block_owner[:, 0]
+    offset = (kept - position * blocks_here)[..., None]
+    to_owner = (offset >= 0) & (offset < blocks_here)
+    to_owner = to_owner & (owner[..., None] == jnp.arange(width, dtype=jnp.int32))
+    lowest = jnp.min(jnp.where(to_owner, offset, blocks_here), axis=1)
+    highest = jnp.max(jnp.where(to_owner, offset, 0), axis=1)
+    send_index = jnp.where(lowest < blocks_here, lowest, 0)
+    send_index = jnp.stack([send_index, highest], axis=2).reshape(layers, width * capacity)
+
+    side = 8
+    half = (POOL - 1) // 2
+    blocked = (layers, blocks_here, BLOCK, head_dim)
+    key_blocks, value_blocks = keys.reshape(blocked), values.reshape(blocked)
+    works = [
+        lambda after, done, first=first: pack(
+            send_index, key_blocks, value_blocks, first, 2, after, done
+        )
+        for first in (0, 2)
+    ]
+    windowed, parcels, arrivals = spread(queries, "ctx", works)
+    windowed = windowed.reshape(layers, rows, head_dim)
+    start = position * shard_len
+    limit = jnp.stack([total_len - window - start, start])
+    scale = head_dim**-0.5 * math.log2(math.e)
+    parcels = gate(parcels, *arrivals)
+    got = lax.all_to_all(parcels, "ctx", split_axis=0, concat_axis=0, tiled=True)
+
+    kept, owner = gate(kept, windowed), gate(owner, windowed)
     source = kept // blocks_here
     entry = jnp.arange(keep_count, dtype=jnp.int32)
     earlier = entry[None, :] < entry[:, None]
@@ -287,34 +343,18 @@
     same_source = source[:, :, None] == source[:, None, :]
     owner_rank = jnp.sum(same_owner & earlier, axis=-1)
     pair_rank = jnp.sum(same_owner & same_source & earlier, axis=-1)
-    slot = owner * capacity + pair_rank
-    send_hit = (source == position)[..., None] & (
-        slot[..., None] == jnp.arange(width * capacity, dtype=jnp.int32)
-    )
-    send_index = jnp.sum(jnp.where(send_hit, (kept % blocks_here)[..., None], 0), axis=1)
     recv_hit = (owner == position)[..., None] & (
         owner_rank[..., None] == jnp.arange(keep_share, dtype=jnp.int32)
     )
     recv_index = jnp.sum(jnp.where(recv_hit, (source * capacity + pair_rank)[..., None], 0), axis=1)
 
-    side = 8
-    half = (POOL - 1) // 2
-    forward = [(i, i + 1) for i in range(width - 1)]
-    backward = [(i + 1, i) for i in range(width - 1)]
-    low = lax.ppermute(keys[:, shard_len - side :], "ctx", forward)
-    high = lax.ppermute(keys[:, :side], "ctx", backward)
-    edges = jnp.concatenate([low, high], axis=1)
-    windowed = spread(queries, "ctx").reshape(layers, rows, head_dim)
-    start = position * shard_len
-    limit = jnp.stack([total_len - window - start, start])
-    scale = head_dim**-0.5 * math.log2(math.e)
     peak, total = local_stats(limit, windowed, keys, group, scale)
-    peak, total = merge_stats(peak.reshape(layers, rows), total.reshape(layers, rows), "ctx")
-
-    blocked = (layers, blocks_here, BLOCK, head_dim)
-    parcels = pack(send_index, keys.reshape(blocked), values.reshape(blocked), total)
-    got = lax.all_to_all(parcels, "ctx", split_axis=0, concat_axis=0, tiled=True)
-
+    ends = jnp.stack([keys[:, shard_len - side :], keys[:, :side]])
+    peak, total, low, high = merge_stats(
+        peak.reshape(layers, rows), total.reshape(layers, rows), ends, "ctx"
+    )
+    low = low.reshape(layers, side, head_dim)
+    edges = jnp.concatenate([low, high.reshape(layers, side, head_dim)], axis=1).astype(keys.dtype)
     factor = (total_len / rows) / total
     mass, edge_mass = local_mass(
         limit, windowed, keys, edges, peak[..., None], factor[..., None], group, scale, total_len
@@ -330,6 +370,7 @@
     shared = total_over(pooled, "head") / KVH
     block_mass = jnp.sum(pooled.reshape(layers, blocks_here, BLOCK), axis=2).astype(jnp.bfloat16)
     sent_mass = jnp.take_along_axis(block_mass, send_index, axis=1)
+    got, sent_mass = lax.optimization_barrier((got, sent_mass))
     got_mass = lax.all_to_all(sent_mass, "ctx", split_axis=1, concat_axis=1, tiled=True)
     kept_mass = jnp.take_along_axis(got_mass, recv_index, axis=1)
 

time: 433 us -> 275 us (0.64)
  Pallas kernels: 157 us -> 44.1 us
  waiting for transfers between devices: 188 us -> 150 us
  starting transfers between devices: 64.2 us -> 31.7 us
  between operations: 1.06 us -> 14.5 us
  other arithmetic: 5.89 us -> 16.4 us
    all_to_all x1, waiting for transfers between devices: 164 us -> 30.9 us  [per_device(): lax.all_to_all(parcels, 'ctx', split_axis=0, concat_axis=0, tiled=True)]
    pallas_call x1 -> x7, Pallas kernels: 129 us -> 8.83 us  [the longest x2 8.82 us: pack(): pl.pallas_call(functools.partial(pack_kernel, first, parts), out_shape=ja...]
    all_gather x0 -> x1, waiting for transfers between devices: none -> 97.5 us  [merge_stats(): every = lax.all_gather(both, axis, axis=0, tiled=False)]
    ppermute x14 -> x10, starting transfers between devices: 36.9 us -> 8.77 us  [the longest x3 3.5 us: spread(): lax.ppermute(piece, axis, [(k * deep + z, (k + dx) % wide * deep + z) for...]
    ppermute x14 -> x10, waiting for transfers between devices: 20.7 us -> 15.7 us  [the longest x4 11.7 us: spread(): lax.ppermute(piece, axis, [(k * deep + z, k * deep + (z + dz) % deep) for...]
  transfers between devices with their start and end apart: 19 -> 16, of which waited for: 10 -> 8; matrix products, arithmetic and copies ran while one was open for 2% -> 9% of each run, Pallas kernels for 33% -> 16%
where the time goes in v2:
time: 275 us; the launch traced here: 272 us
  waiting for transfers between devices  150 us (55%)
  Pallas kernels  44.1 us (16%)
  starting transfers between devices  31.7 us (12%)
  other arithmetic  16.4 us (6%)
  local copies, waits for them, and re-layouts  15 us (5%)
  between operations  14.5 us (5%)
    all_gather x1, waiting for transfers between devices, merge_stats(): every = lax.all_gather(both, axis, axis=0, tiled=False)  97.5 us
    all_to_all x1, waiting for transfers between devices, per_device(): lax.all_to_all(parcels, 'ctx', split_axis=0, concat_axis=0, tiled=True)  30.9 us
    pallas_call x1, Pallas kernels, local_stats(): pl.pallas_call(functools.partial(stats_kernel, group, scale), out_shape=(...  15.9 us
    pallas_call x1, Pallas kernels, local_mass(): pl.pallas_call(functools.partial(mass_kernel, group, scale, shard_len, to...  15.7 us
    all_to_all x1, starting transfers between devices, per_device(): lax.all_to_all(sent_mass, 'ctx', split_axis=1, concat_axis=1, tiled=True)  11.8 us
    ppermute x4, waiting for transfers between devices, spread(): lax.ppermute(piece, axis, [(k * deep + z, k * deep + (z + dz) % deep) for...  11.7 us
    pallas_call x2, Pallas kernels, pack(): pl.pallas_call(functools.partial(pack_kernel, first, parts), out_shape=ja...  8.82 us
    all_to_all x1, starting transfers between devices, per_device(): lax.all_to_all(parcels, 'ctx', split_axis=0, concat_axis=0, tiled=True)  6.91 us
  transfers between devices with their start and end apart: 16, of which 8 were waited for; matrix products, arithmetic and copies ran while one was open for 9% of the time, Pallas kernels for 16%

profile of v2, /device:TPU:2, one launch (start us, length us, event | category | flops | bytes accessed | tf_op | source)
XLA Modules:
  0.0 271.9 jit_solution(3001728462002382586)
XLA Ops:
  7.2 0.9 slice_bitcast_fusion.1
  8.1 0.7 collective-permute-start
  8.8 0.7 collective-permute-start.1
  9.4 0.7 collective-permute-start.2
  10.1 0.7 copy.58
  10.8 0.7 compare_and_fusion.2
  11.5 0.2 select_reduce_fusion.1
  11.7 0.9 fusion.13.rest_0_
  12.6 0.7 collective-permute-start.3
  13.3 0.7 collective-permute-start.4
  14.0 0.7 collective-permute-start.5
  14.7 0.7 reshape.195.index_ref
  15.4 4.4 %pack.2.refs_1_.rest_1_ = bf16[64,4,128,128]{3,2,1,0:T(8,128)(2,1)} custom-call(s32[2,64]{1,0:T(2,128)} %reshape.195.index_ref, bf16[2,64,128,128]{3,2,1,0:T(8,128)(2,1)} %bitcast.72, bf16[2,64,128,128]{3,2,1,0:T(8,128)(2,1)} %bitcast.77, bf16[32,8,128]{2,1,0:T(8,128)(2,1)} %copy-done.1), custom_call_target="tpu_custom_call" | custom-call | bytes 8388608 | tf_op jit(solution)/shard_map/pack/pallas_call | solution.py:35
  19.8 0.7 add_select_fusion.refs_0_
  20.5 1.3 collective-permute-start.6
  21.8 4.5 %pack.3.refs_1_.refs_0_ = bf16[64,4,128,128]{3,2,1,0:T(8,128)(2,1)} custom-call(s32[2,64]{1,0:T(2,128)} %reshape.195.index_ref, bf16[2,64,128,128]{3,2,1,0:T(8,128)(2,1)} %bitcast.73, bf16[2,64,128,128]{3,2,1,0:T(8,128)(2,1)} %bitcast.78, bf16[32,8,128]{2,1,0:T(8,128)(2,1)} %gate.5.rest_0_, ...), custom_call_target="tpu_custom_call", output_to_operand_aliasing={{}: (4, {})} | custom-call | bytes 8388608 | tf_op jit(solution)/shard_map/pack/pallas_call | solution.py:35
  26.3 11.7 %collective-permute-done.6 = bf16[32,8,128]{2,1,0:T(8,128)(2,1)S(1)} collective-permute-done((bf16[32,8,128]{2,1,0:T(8,128)(2,1)}, bf16[32,8,128]{2,1,0:T(8,128)(2,1)S(1)}, u32[]{:S(2)}, u32[]{:S(2)}) %collective-permute-start.6) | collective-permute-done | bytes 65568 | tf_op jit(solution)/shard_map/ppermute | solution.py:243
  38.0 0.6 broadcast_select_fusion.refs_0_
  38.6 1.4 collective-permute-start.7
  40.1 2.1 collective-permute-start.9
  42.1 1.0 collective-permute-done.7.refs_1_
  43.1 2.9 %collective-permute-done.8.refs_2_ = bf16[32,8,128]{2,1,0:T(8,128)(2,1)S(1)} collective-permute-done((bf16[32,8,128]{2,1,0:T(8,128)(2,1)}, bf16[32,8,128]{2,1,0:T(8,128)(2,1)S(1)}, u32[]{:S(2)}, u32[]{:S(2)}) %collective-permute-start.8) | collective-permute-done | bytes 65568 | tf_op jit(solution)/shard_map/ppermute | solution.py:256
  46.1 0.6 copy-done.5
  46.7 0.6 copy-done.7
  47.3 6.9 %all-to-all-start = ((bf16[64,4,128,128]{3,2,1,0:T(8,128)(2,1)}), bf16[64,4,128,128]{3,2,1,0:T(8,128)(2,1)}, u32[]{:S(2)}, u32[]{:S(2)}) async-start(bf16[64,4,128,128]{3,2,1,0:T(8,128)(2,1)} %gate.9), calls=%async_computation | async-start | bytes 16777216 | tf_op jit(solution)/shard_map/all_to_all | solution.py:336
  54.4 0.7 slice_bitcast_fusion.5
  55.1 0.6 pad_add_fusion.1.limit_ref
  55.8 0.8 pad_maximum_fusion
  56.6 15.9 %stats.1 = (f32[2,512,1]{2,1,0:T(8,128)}, f32[2,512,1]{2,1,0:T(8,128)}) custom-call(s32[2]{0:T(128)} %pad_add_fusion.1.limit_ref, bf16[2,512,128]{2,1,0:T(8,128)(2,1)} %bitcast.79, bf16[2,8192,128]{2,1,0:T(8,128)(2,1)} %bitcast.75), custom_call_target="tpu_custom_call" | custom-call | flops 2147483648 | bytes 4194304 | tf_op jit(solution)/shard_map/stats/pallas_call | solution.py:142
  72.5 1.2 reduce
  73.8 1.3 reduce.1
  75.0 1.2 concatenate.18
  76.4 0.6 copy.59
  77.2 0.7 and_select_fusion
  77.9 2.1 convert_reduce_fusion.1
  80.0 0.7 broadcast_compare_fusion
  80.7 0.7 multiply_add_fusion
  81.4 0.1 select_reduce_fusion.2.index_ref
  81.6 97.5 %all-gather.3.cloned.1.call-done = f32[512,512]{1,0:T(8,128)} async-done(((f32[16,512]{1,0:T(8,128)}), f32[512,512]{1,0:T(8,128)}) %all-gather.3.cloned.1.call-update) | async-done | bytes 1048592 | tf_op jit(solution)/shard_map/all_gather | solution.py:277
  179.1 1.1 slice_reduce_fusion
  180.2 1.4 fusion.1
  181.6 1.0 copy.39.factor_ref
  182.6 1.0 copy.38.peak_ref
  183.7 0.7 dynamic-slice_convert_fusion.1
  184.4 0.6 pad_maximum_fusion.3.edge_ref
  185.0 15.7 %mass.1 = (f32[2,1,8192]{2,1,0:T(1,128)}, f32[2,1,16]{2,1,0:T(1,128)}) custom-call(s32[2]{0:T(128)} %pad_add_fusion.1.limit_ref, bf16[2,512,128]{2,1,0:T(8,128)(2,1)} %bitcast.82, bf16[2,8192,128]{2,1,0:T(8,128)(2,1)} %bitcast.76, bf16[2,16,128]{2,1,0:T(8,128)(2,1)} %pad_maximum_fusion.3.edge_ref, f32[2,512,1]{2,1,0:T(8,128)} %copy.38.peak_ref, ...), custom_call_target="tpu_custom_call" | custom-call | flops 2147483648 | bytes 4194304 | tf_op jit(solution)/shard_map/mass/pallas_call | solution.py:195
  200.7 0.9 copy.57
  201.6 0.8 fusion.23
  202.4 0.5 fusion.15
  203.1 1.1 collective-permute-done.10
  204.3 1.9 collective-permute-start.11
  206.3 1.5 gather_fusion
  207.9 0.8 collective-permute-done.11
  208.7 2.2 collective-permute-start.12
  210.8 0.7 copy.43
  211.5 30.9 %all-to-all-done.got_ref = bf16[64,4,128,128]{3,2,1,0:T(8,128)(2,1)} async-done(((bf16[64,4,128,128]{3,2,1,0:T(8,128)(2,1)}), bf16[64,4,128,128]{3,2,1,0:T(8,128)(2,1)}, u32[]{:S(2)}, u32[]{:S(2)}) %all-to-all-start) | async-done | bytes 8388640 | tf_op jit(solution)/shard_map/all_to_all | solution.py:336
  242.6 0.6 copy.41
  243.2 11.8 %all-to-all-start.1 = ((bf16[2,32,2]{2,0,1:T(2,128)(2,1)}), bf16[2,32,2]{2,0,1:T(2,128)(2,1)S(1)}, u32[]{:S(2)}, u32[]{:S(2)}) async-start(bf16[2,32,2]{2,0,1:T(2,128)(2,1)} %copy.41), calls=%async_computation.1 | async-start | bytes 32768 | tf_op jit(solution)/shard_map/all_to_all | solution.py:374
  255.0 0.7 add_multiply_fusion
  255.7 3.6 %unpack.1 = (bf16[2,16,128,128]{3,2,1,0:T(8,128)(2,1)}, bf16[2,16,128,128]{3,2,1,0:T(8,128)(2,1)}) custom-call(s32[2,16]{1,0:T(2,128)} %copy-done.11, bf16[64,4,128,128]{3,2,1,0:T(8,128)(2,1)} %all-to-all-done.got_ref), custom_call_target="tpu_custom_call" | custom-call | bytes 4194304 | tf_op jit(solution)/shard_map/unpack/pallas_call | solution.py:89
  259.3 4.2 %all-to-all-done.1 = bf16[2,32,2]{2,0,1:T(2,128)(2,1)S(1)} async-done(((bf16[2,32,2]{2,0,1:T(2,128)(2,1)}), bf16[2,32,2]{2,0,1:T(2,128)(2,1)S(1)}, u32[]{:S(2)}, u32[]{:S(2)}) %all-to-all-start.1) | async-done | bytes 288 | tf_op jit(solution)/shard_map/all_to_all | solution.py:374
  263.6 0.1 all_to_all.14
  263.7 0.7 gather_fusion.1
  264.5 0.5 and_select_fusion.1
  (69 shorter events, 1.3 us)
Async XLA Ops:
  8.1 3.6 %collective-permute-start = (bf16[32,8,128]{2,1,0:T(8,128)(2,1)S(1)}, bf16[32,8,128]{2,1,0:T(8,128)(2,1)S(1)}, u32[]{:S(2)}, u32[]{:S(2)}) collective-permute-start(bf16[32,8,128]{2,1,0:T(8,128)(2,1)S(1)} %get-tuple-element.57), channel_id=1, source_target_pairs={{248,56},{249,57},{250,58},{251,59},{252,60},{253,61},{254,62},{25... | collective-permute-start | bytes 196616 | tf_op jit(solution)/shard_map/ppermute | solution.py:237
  8.8 3.0 %collective-permute-start.1 = (bf16[32,8,128]{2,1,0:T(8,128)(2,1)S(1)}, bf16[32,8,128]{2,1,0:T(8,128)(2,1)S(1)}, u32[]{:S(2)}, u32[]{:S(2)}) collective-permute-start(bf16[32,8,128]{2,1,0:T(8,128)(2,1)S(1)} %get-tuple-element.55), channel_id=1, source_target_pairs={{248,120},{249,121},{250,122},{251,123},{252,124},{253,125},{254,1... | collective-permute-start | bytes 196616 | tf_op jit(solution)/shard_map/ppermute | solution.py:237
  9.4 2.3 collective-permute-start.2
  10.8 9.0 %copy-start.9 = (s32[2,1,512]{2,0,1:T(2,128)}, s32[2,1,512]{2,0,1:T(2,128)S(1)}, u32[]{:S(2)}) copy-start(s32[2,1,512]{2,0,1:T(2,128)S(1)} %copy.58) | copy-start | bytes 12292
  12.6 2.8 %copy-start.1 = (bf16[32,8,128]{2,1,0:T(8,128)(2,1)}, bf16[32,8,128]{2,1,0:T(8,128)(2,1)S(1)}, u32[]{:S(2)}) copy-start(bf16[32,8,128]{2,1,0:T(8,128)(2,1)S(1)} %fusion.13.rest_0_) | copy-start | bytes 196612
  12.6 7.2 %collective-permute-start.3 = (bf16[32,8,128]{2,1,0:T(8,128)(2,1)S(1)}, bf16[32,8,128]{2,1,0:T(8,128)(2,1)S(1)}, u32[]{:S(2)}, u32[]{:S(2)}) collective-permute-start(bf16[32,8,128]{2,1,0:T(8,128)(2,1)S(1)} %fusion.13.rest_0_), channel_id=1, source_target_pairs={{56,8},{120,72},{184,136},{248,200},{57,9},{121,73},{185,137},{249... | collective-permute-start | bytes 196616 | tf_op jit(solution)/shard_map/ppermute | solution.py:243
  13.3 6.5 %collective-permute-start.4 = (bf16[32,8,128]{2,1,0:T(8,128)(2,1)S(1)}, bf16[32,8,128]{2,1,0:T(8,128)(2,1)S(1)}, u32[]{:S(2)}, u32[]{:S(2)}) collective-permute-start(bf16[32,8,128]{2,1,0:T(8,128)(2,1)S(1)} %fusion.13.rest_0_), channel_id=1, source_target_pairs={{56,24},{120,88},{184,152},{248,216},{57,25},{121,89},{185,153},{2... | collective-permute-start | bytes 196616 | tf_op jit(solution)/shard_map/ppermute | solution.py:243
  14.0 5.9 %collective-permute-start.5 = (bf16[32,8,128]{2,1,0:T(8,128)(2,1)S(1)}, bf16[32,8,128]{2,1,0:T(8,128)(2,1)S(1)}, u32[]{:S(2)}, u32[]{:S(2)}) collective-permute-start(bf16[32,8,128]{2,1,0:T(8,128)(2,1)S(1)} %fusion.13.rest_0_), channel_id=1, source_target_pairs={{56,40},{120,104},{184,168},{248,232},{57,41},{121,105},{185,169},... | collective-permute-start | bytes 196616 | tf_op jit(solution)/shard_map/ppermute | solution.py:243
  20.5 17.5 %collective-permute-start.6 = (bf16[32,8,128]{2,1,0:T(8,128)(2,1)}, bf16[32,8,128]{2,1,0:T(8,128)(2,1)S(1)}, u32[]{:S(2)}, u32[]{:S(2)}) collective-permute-start(bf16[32,8,128]{2,1,0:T(8,128)(2,1)} %gate.5.rest_0_), channel_id=1, source_target_pairs={{56,0},{8,16},{24,32},{40,48},{120,64},{72,80},{88,96},{104,112},{... | collective-permute-start | bytes 196616 | tf_op jit(solution)/shard_map/ppermute | solution.py:243
  21.8 16.2 %copy-start = (bf16[32,8,128]{2,1,0:T(8,128)(2,1)S(1)}, bf16[32,8,128]{2,1,0:T(8,128)(2,1)}, u32[]{:S(2)}) copy-start(bf16[32,8,128]{2,1,0:T(8,128)(2,1)} %gate.5.rest_0_) | copy-start | bytes 196612
  38.6 4.5 %collective-permute-start.7 = (bf16[32,8,128]{2,1,0:T(8,128)(2,1)}, bf16[32,8,128]{2,1,0:T(8,128)(2,1)S(1)}, u32[]{:S(2)}, u32[]{:S(2)}) collective-permute-start(bf16[32,8,128]{2,1,0:T(8,128)(2,1)} %gate.6), channel_id=1, source_target_pairs={{0,64},{8,72},{16,80},{24,88},{32,96},{40,104},{48,112},{56,120},{... | collective-permute-start | bytes 196616 | tf_op jit(solution)/shard_map/ppermute | solution.py:256
  40.1 6.0 %collective-permute-start.8 = (bf16[32,8,128]{2,1,0:T(8,128)(2,1)}, bf16[32,8,128]{2,1,0:T(8,128)(2,1)S(1)}, u32[]{:S(2)}, u32[]{:S(2)}) collective-permute-start(bf16[32,8,128]{2,1,0:T(8,128)(2,1)} %gate.6), channel_id=1, source_target_pairs={{0,128},{8,136},{16,144},{24,152},{32,160},{40,168},{48,176},{56,1... | collective-permute-start | bytes 196616 | tf_op jit(solution)/shard_map/ppermute | solution.py:256
  40.1 6.0 %collective-permute-start.9 = (bf16[32,8,128]{2,1,0:T(8,128)(2,1)}, bf16[32,8,128]{2,1,0:T(8,128)(2,1)S(1)}, u32[]{:S(2)}, u32[]{:S(2)}) collective-permute-start(bf16[32,8,128]{2,1,0:T(8,128)(2,1)} %gate.6), channel_id=1, source_target_pairs={{0,192},{8,200},{16,208},{24,216},{32,224},{40,232},{48,240},{56,2... | collective-permute-start | bytes 196616 | tf_op jit(solution)/shard_map/ppermute | solution.py:256
  43.1 2.9 %copy-start.3 = (bf16[32,8,128]{2,1,0:T(8,128)(2,1)}, bf16[32,8,128]{2,1,0:T(8,128)(2,1)S(1)}, u32[]{:S(2)}) copy-start(bf16[32,8,128]{2,1,0:T(8,128)(2,1)S(1)} %collective-permute-done.7.refs_1_) | copy-start | bytes 196612
  46.1 0.6 copy-start.5
  46.7 0.6 copy-start.7
  47.3 8.4 %copy-start.2 = (bf16[32,8,128]{2,1,0:T(8,128)(2,1)S(1)}, bf16[32,8,128]{2,1,0:T(8,128)(2,1)}, u32[]{:S(2)}) copy-start(bf16[32,8,128]{2,1,0:T(8,128)(2,1)} %gate.6) | copy-start | bytes 196612
  47.3 8.4 %copy-start.4 = (bf16[32,8,128]{2,1,0:T(8,128)(2,1)S(1)}, bf16[32,8,128]{2,1,0:T(8,128)(2,1)}, u32[]{:S(2)}) copy-start(bf16[32,8,128]{2,1,0:T(8,128)(2,1)} %copy-done.3) | copy-start | bytes 196612
  47.3 8.4 %copy-start.6 = (bf16[32,8,128]{2,1,0:T(8,128)(2,1)S(1)}, bf16[32,8,128]{2,1,0:T(8,128)(2,1)}, u32[]{:S(2)}) copy-start(bf16[32,8,128]{2,1,0:T(8,128)(2,1)} %copy-done.5) | copy-start | bytes 196612
  47.3 8.4 %copy-start.8 = (bf16[32,8,128]{2,1,0:T(8,128)(2,1)S(1)}, bf16[32,8,128]{2,1,0:T(8,128)(2,1)}, u32[]{:S(2)}) copy-start(bf16[32,8,128]{2,1,0:T(8,128)(2,1)} %copy-done.7) | copy-start | bytes 196612
  47.3 195.1 %all-to-all-start = ((bf16[64,4,128,128]{3,2,1,0:T(8,128)(2,1)}), bf16[64,4,128,128]{3,2,1,0:T(8,128)(2,1)}, u32[]{:S(2)}, u32[]{:S(2)}) async-start(bf16[64,4,128,128]{3,2,1,0:T(8,128)(2,1)} %gate.9), calls=%async_computation | async-start | bytes 16777216 | tf_op jit(solution)/shard_map/all_to_all | solution.py:336
  54.2 124.8 %all-gather.3.cloned.1.call-start = ((), (), s32[]{:S(2)}) async-start(), calls=%async_computation.2 | async-start | bytes 1081344 | tf_op jit(solution)/shard_map/all_gather | solution.py:277
  56.6 19.8 %copy-start.13 = (s32[2,1,512]{2,1,0:T(1,128)S(1)}, s32[2,1,512]{2,1,0:T(1,128)}, u32[]{:S(2)}) copy-start(s32[2,1,512]{2,1,0:T(1,128)} %param.8) | copy-start | bytes 12292
  81.6 121.4 %copy-start.11 = (s32[2,16]{1,0:T(2,128)}, s32[2,16]{1,0:T(2,128)S(1)}, u32[]{:S(2)}) copy-start(s32[2,16]{1,0:T(2,128)S(1)} %select_reduce_fusion.2.index_ref) | copy-start | bytes 388
  185.0 25.8 %copy-start.10 = (s32[2,64]{1,0:T(2,128)S(1)}, s32[2,64]{1,0:T(2,128)}, u32[]{:S(2)}) copy-start(s32[2,64]{1,0:T(2,128)} %reshape.195.index_ref) | copy-start | bytes 1540
  202.9 1.3 collective-permute-start.10
  204.3 4.4 %collective-permute-start.11 = (f32[2,8192]{1,0:T(2,128)S(1)}, f32[2,8192]{1,0:T(2,128)S(1)}, u32[]{:S(2)}, u32[]{:S(2)}) collective-permute-start(f32[2,8192]{1,0:T(2,128)S(1)} %add.138), channel_id=1, source_target_pairs={{0,2},{1,3},{2,0},{3,1},{4,6},{5,7},{6,4},{7,5},{8,10},{9,11},{10,... | collective-permute-start | bytes 196616 | tf_op jit(solution)/shard_map/ppermute | solution.py:292
  208.7 46.3 %collective-permute-start.12 = (f32[2,8192]{1,0:T(2,128)S(1)}, f32[2,8192]{1,0:T(2,128)S(1)}, u32[]{:S(2)}, u32[]{:S(2)}) collective-permute-start(f32[2,8192]{1,0:T(2,128)S(1)} %add.139), channel_id=1, source_target_pairs={{0,4},{1,5},{2,6},{3,7},{4,0},{5,1},{6,2},{7,3},{8,12},{9,13},{10,... | collective-permute-start | bytes 196616 | tf_op jit(solution)/shard_map/ppermute | solution.py:292
  243.2 20.4 %all-to-all-start.1 = ((bf16[2,32,2]{2,0,1:T(2,128)(2,1)}), bf16[2,32,2]{2,0,1:T(2,128)(2,1)S(1)}, u32[]{:S(2)}, u32[]{:S(2)}) async-start(bf16[2,32,2]{2,0,1:T(2,128)(2,1)} %copy.41), calls=%async_computation.1 | async-start | bytes 32768 | tf_op jit(solution)/shard_map/all_to_all | solution.py:374
  255.7 8.8 %copy-start.12 = (s32[2,16]{1,0:T(2,128)S(1)}, s32[2,16]{1,0:T(2,128)}, u32[]{:S(2)}) copy-start(s32[2,16]{1,0:T(2,128)} %copy-done.11) | copy-start | bytes 388
Sparse Core Ops, SparseCore 0:
  76.4 102.6 all-gather.2

commit v3 on v2

--- a/solution.py
+++ b/solution.py
@@ -369,10 +369,38 @@
     pooled = pooled / POOL
     shared = total_over(pooled, "head") / KVH
     block_mass = jnp.sum(pooled.reshape(layers, blocks_here, BLOCK), axis=2).astype(jnp.bfloat16)
-    sent_mass = jnp.take_along_axis(block_mass, send_index, axis=1)
-    got, sent_mass = lax.optimization_barrier((got, sent_mass))
-    got_mass = lax.all_to_all(sent_mass, "ctx", split_axis=1, concat_axis=1, tiled=True)
-    kept_mass = jnp.take_along_axis(got_mass, recv_index, axis=1)
+    wide, deep = grid_of("ctx")
+    across = position // deep
+    sent_mass = jnp.take_along_axis(block_mass, send_index, axis=1).astype(jnp.float32)
+    rows_mass = [sent_mass] + [
+        lax.ppermute(
+            sent_mass,
+            "ctx",
+            [(k * deep + z, (k + dx) % wide * deep + z) for k in range(wide) for z in range(deep)],
+        )
+        for dx in range(1, wide)
+    ]
+    rows_mass = jnp.stack(rows_mass).reshape(wide, layers, wide, deep, capacity)
+    mine = jnp.arange(wide, dtype=jnp.int32)[:, None, None] == across
+    rows_mass = jnp.sum(jnp.where(mine, rows_mass, 0.0), axis=2)
+    rows_mass = gate(rows_mass.reshape(1, -1), shared)
+
+    def from_before(x, dz):
+        pairs = [(k * deep + z, k * deep + (z + dz) % deep) for k in range(wide) for z in range(deep)]
+        return lax.ppermute(x, "ctx", pairs)
+
+    even = [rows_mass] + [from_before(rows_mass, dz) for dz in range(2, deep, 2)]
+    even = jnp.concatenate(even, axis=0)
+    got, even = lax.optimization_barrier((got, even))
+    got_mass = jnp.stack([even, from_before(even, 1)], axis=1)
+    layer = jnp.arange(layers, dtype=jnp.int32)[:, None]
+    from_row, from_column = recv_index // capacity % deep, recv_index // capacity // deep
+    along = position % deep
+    mass_index = (along - from_row) % deep * wide + (across - from_column) % wide
+    mass_index = (mass_index * layers + layer) * deep + along
+    mass_index = mass_index * capacity + recv_index % capacity
+    wanted = mass_index[..., None] == jnp.arange(got_mass.size, dtype=jnp.int32)
+    kept_mass = jnp.sum(jnp.where(wanted, got_mass.reshape(-1), 0.0), axis=2).astype(jnp.bfloat16)
 
     compact_keys, compact_values = unpack(recv_index, got)
     share = (layers, heads_here, keep_share * BLOCK, head_dim)

time: 275 us -> 261 us (0.949)
  waiting for transfers between devices: 150 us -> 131 us
  starting transfers between devices: 31.7 us -> 35.5 us
    all_to_all x1, waiting for transfers between devices: 30.9 us -> 0.01 us  [per_device(): lax.all_to_all(parcels, 'ctx', split_axis=0, concat_axis=0, tiled=True)]
    ppermute x0 -> x7, waiting for transfers between devices: none -> 18.5 us  [the longest x4 18 us: from_before(): return lax.ppermute(x, 'ctx', pairs)]
    ppermute x0 -> x7, starting transfers between devices: none -> 16.1 us  [the longest x4 10.3 us: from_before(): return lax.ppermute(x, 'ctx', pairs)]
    all_to_all x1 -> x0, starting transfers between devices: 11.8 us -> none  [per_device(): lax.all_to_all(sent_mass, 'ctx', split_axis=1, concat_axis=1, tiled=True)]
    all_gather x1, waiting for transfers between devices: 97.5 us -> 90.2 us  [merge_stats(): every = lax.all_gather(both, axis, axis=0, tiled=False)]
    all_to_all x1 -> x0, waiting for transfers between devices: 4.23 us -> none  [per_device(): lax.all_to_all(sent_mass, 'ctx', split_axis=1, concat_axis=1, tiled=True)]
  transfers between devices with their start and end apart: 16 -> 22, of which waited for: 8 -> 9; matrix products, arithmetic and copies ran while one was open for 9% -> 11% of each run, Pallas kernels for 16% -> 17%
where the time goes in v3:
time: 261 us; the launch traced here: 257 us
  waiting for transfers between devices  131 us (50%)
  Pallas kernels  44 us (17%)
  starting transfers between devices  35.5 us (14%)
  other arithmetic  17.4 us (7%)
  between operations  14.6 us (6%)
  local copies, waits for them, and re-layouts  14.5 us (6%)
    all_gather x1, waiting for transfers between devices, merge_stats(): every = lax.all_gather(both, axis, axis=0, tiled=False)  90.2 us
    ppermute x4, waiting for transfers between devices, from_before(): return lax.ppermute(x, 'ctx', pairs)  18 us
    pallas_call x1, Pallas kernels, local_stats(): pl.pallas_call(functools.partial(stats_kernel, group, scale), out_shape=(...  15.9 us
    pallas_call x1, Pallas kernels, local_mass(): pl.pallas_call(functools.partial(mass_kernel, group, scale, shard_len, to...  15.7 us
    ppermute x4, waiting for transfers between devices, spread(): lax.ppermute(piece, axis, [(k * deep + z, k * deep + (z + dz) % deep) for...  12.6 us
    ppermute x4, starting transfers between devices, from_before(): return lax.ppermute(x, 'ctx', pairs)  10.3 us
    pallas_call x2, Pallas kernels, pack(): pl.pallas_call(functools.partial(pack_kernel, first, parts), out_shape=ja...  8.85 us
    all_to_all x1, starting transfers between devices, per_device(): lax.all_to_all(parcels, 'ctx', split_axis=0, concat_axis=0, tiled=True)  7.94 us
  transfers between devices with their start and end apart: 22, of which 9 were waited for; matrix products, arithmetic and copies ran while one was open for 11% of the time, Pallas kernels for 17%

profile of v3, /device:TPU:2, one launch (start us, length us, event | category | flops | bytes accessed | tf_op | source)
XLA Modules:
  0.0 256.7 jit_solution(5854413452942568653)
XLA Ops:
  7.2 0.9 slice_bitcast_fusion.1
  8.1 0.7 collective-permute-start.2
  8.8 0.7 collective-permute-start
  9.4 0.7 collective-permute-start.1
  10.1 0.7 copy.76
  10.8 0.7 compare_and_fusion.2
  11.7 0.9 fusion.13.rest_0_
  12.6 0.7 collective-permute-start.5
  13.3 0.7 collective-permute-start.3
  14.0 0.7 collective-permute-start.4
  14.7 0.7 reshape.385.index_ref
  15.4 4.4 %pack.2.refs_1_.rest_1_ = bf16[64,4,128,128]{3,2,1,0:T(8,128)(2,1)} custom-call(s32[2,64]{1,0:T(2,128)} %reshape.385.index_ref, bf16[2,64,128,128]{3,2,1,0:T(8,128)(2,1)} %bitcast.76, bf16[2,64,128,128]{3,2,1,0:T(8,128)(2,1)} %bitcast.81, bf16[32,8,128]{2,1,0:T(8,128)(2,1)} %copy-done.1), custom_call_target="tpu_custom_call" | custom-call | bytes 8388608 | tf_op jit(solution)/shard_map/pack/pallas_call | solution.py:35
  19.9 0.7 add_select_fusion.refs_0_
  20.5 1.3 collective-permute-start.6
  21.9 4.4 %pack.3.refs_1_.refs_0_ = bf16[64,4,128,128]{3,2,1,0:T(8,128)(2,1)} custom-call(s32[2,64]{1,0:T(2,128)} %reshape.385.index_ref, bf16[2,64,128,128]{3,2,1,0:T(8,128)(2,1)} %bitcast.77, bf16[2,64,128,128]{3,2,1,0:T(8,128)(2,1)} %bitcast.82, bf16[32,8,128]{2,1,0:T(8,128)(2,1)} %gate.6.rest_0_, ...), custom_call_target="tpu_custom_call", output_to_operand_aliasing={{}: (4, {})} | custom-call | bytes 8388608 | tf_op jit(solution)/shard_map/pack/pallas_call | solution.py:35
  26.3 12.6 %collective-permute-done.6 = bf16[32,8,128]{2,1,0:T(8,128)(2,1)S(1)} collective-permute-done((bf16[32,8,128]{2,1,0:T(8,128)(2,1)}, bf16[32,8,128]{2,1,0:T(8,128)(2,1)S(1)}, u32[]{:S(2)}, u32[]{:S(2)}) %collective-permute-start.6) | collective-permute-done | bytes 65568 | tf_op jit(solution)/shard_map/ppermute | solution.py:243
  38.9 0.6 broadcast_select_fusion.refs_0_
  39.6 2.0 collective-permute-start.7
  41.5 4.0 %collective-permute-done.8.refs_2_ = bf16[32,8,128]{2,1,0:T(8,128)(2,1)S(1)} collective-permute-done((bf16[32,8,128]{2,1,0:T(8,128)(2,1)}, bf16[32,8,128]{2,1,0:T(8,128)(2,1)S(1)}, u32[]{:S(2)}, u32[]{:S(2)}) %collective-permute-start.8) | collective-permute-done | bytes 65568 | tf_op jit(solution)/shard_map/ppermute | solution.py:256
  45.5 1.2 collective-permute-done.7.refs_1_
  46.7 0.6 copy-done.7
  47.4 7.9 %all-to-all-start = ((bf16[64,4,128,128]{3,2,1,0:T(8,128)(2,1)}), bf16[64,4,128,128]{3,2,1,0:T(8,128)(2,1)}, u32[]{:S(2)}, u32[]{:S(2)}) async-start(bf16[64,4,128,128]{3,2,1,0:T(8,128)(2,1)} %gate.10), calls=%async_computation | async-start | bytes 16777216 | tf_op jit(solution)/shard_map/all_to_all | solution.py:336
  55.5 0.7 slice_bitcast_fusion.5
  56.2 0.6 pad_add_fusion.1.limit_ref
  56.9 0.8 pad_maximum_fusion
  57.6 15.9 %stats.1 = (f32[2,512,1]{2,1,0:T(8,128)}, f32[2,512,1]{2,1,0:T(8,128)}) custom-call(s32[2]{0:T(128)} %pad_add_fusion.1.limit_ref, bf16[2,512,128]{2,1,0:T(8,128)(2,1)} %bitcast.83, bf16[2,8192,128]{2,1,0:T(8,128)(2,1)} %bitcast.79), custom_call_target="tpu_custom_call" | custom-call | flops 2147483648 | bytes 4194304 | tf_op jit(solution)/shard_map/stats/pallas_call | solution.py:142
  73.6 1.2 reduce
  74.8 1.3 reduce.1
  76.1 1.2 concatenate.41
  77.4 0.6 copy.77
  78.5 0.7 and_select_fusion.1
  79.2 2.1 convert_reduce_fusion.1
  81.3 0.7 broadcast_compare_fusion
  82.0 0.7 multiply_add_fusion
  82.7 90.2 %all-gather.3.cloned.1.call-done = f32[512,512]{1,0:T(8,128)} async-done(((f32[16,512]{1,0:T(8,128)}), f32[512,512]{1,0:T(8,128)}) %all-gather.3.cloned.1.call-update) | async-done | bytes 1048592 | tf_op jit(solution)/shard_map/all_gather | solution.py:277
  172.9 0.7 dynamic-slice_convert_fusion.1
  173.6 1.1 slice_reduce_fusion
  174.7 1.0 copy.52.peak_ref
  175.8 1.5 fusion.1
  177.3 1.0 copy.53.factor_ref
  178.3 0.6 pad_maximum_fusion.3.edge_ref
  178.9 15.7 %mass.1 = (f32[2,1,8192]{2,1,0:T(1,128)}, f32[2,1,16]{2,1,0:T(1,128)}) custom-call(s32[2]{0:T(128)} %pad_add_fusion.1.limit_ref, bf16[2,512,128]{2,1,0:T(8,128)(2,1)} %bitcast.86, bf16[2,8192,128]{2,1,0:T(8,128)(2,1)} %bitcast.80, bf16[2,16,128]{2,1,0:T(8,128)(2,1)} %pad_maximum_fusion.3.edge_ref, f32[2,512,1]{2,1,0:T(8,128)} %copy.52.peak_ref, ...), custom_call_target="tpu_custom_call" | custom-call | flops 2147483648 | bytes 4194304 | tf_op jit(solution)/shard_map/mass/pallas_call | solution.py:195
  194.6 0.9 copy.75
  195.5 0.8 fusion.30
  197.0 1.5 gather_fusion
  198.6 2.8 %collective-permute-start.15 = (f32[2,64]{1,0:T(2,128)S(1)}, f32[2,64]{1,0:T(2,128)S(1)}, u32[]{:S(2)}, u32[]{:S(2)}) collective-permute-start(f32[2,64]{1,0:T(2,128)S(1)} %fusion.28), channel_id=1, source_target_pairs={{0,192},{8,200},{16,208},{24,216},{32,224},{40,232},{48,240},{56,2... | collective-permute-start | bytes 1544 | tf_op jit(solution)/shard_map/ppermute | solution.py:376
  201.3 0.9 collective-permute-start.14
  202.2 2.2 collective-permute-start.13
  204.7 0.9 collective-permute-start.11
  205.9 0.5 collective-permute-done.14
  206.9 2.4 collective-permute-done.11
  209.3 3.0 %collective-permute-start.12 = (f32[2,8192]{1,0:T(2,128)S(1)}, f32[2,8192]{1,0:T(2,128)S(1)}, u32[]{:S(2)}, u32[]{:S(2)}) collective-permute-start(f32[2,8192]{1,0:T(2,128)S(1)} %add.202), channel_id=1, source_target_pairs={{0,4},{1,5},{2,6},{3,7},{4,0},{5,1},{6,2},{7,3},{8,12},{9,13},{10,... | collective-permute-start | bytes 196616 | tf_op jit(solution)/shard_map/ppermute | solution.py:292
  212.6 0.7 reshape.393.refs_0_
  213.2 2.0 collective-permute-done.12
  215.2 0.7 add_multiply_fusion.refs_1_
  215.8 5.9 %collective-permute-start.18 = (f32[1,128]{1,0:T(1,128)}, f32[1,128]{1,0:T(1,128)S(1)}, u32[]{:S(2)}, u32[]{:S(2)}) collective-permute-start(f32[1,128]{1,0:T(1,128)} %gate.11), channel_id=1, source_target_pairs={{0,48},{8,56},{16,0},{24,8},{32,16},{40,24},{48,32},{56,40},{64,11... | collective-permute-start | bytes 1544 | tf_op jit(solution)/shard_map/ppermute | solution.py:390
  221.9 2.9 %collective-permute-start.16 = (f32[1,128]{1,0:T(1,128)}, f32[1,128]{1,0:T(1,128)S(1)}, u32[]{:S(2)}, u32[]{:S(2)}) collective-permute-start(f32[1,128]{1,0:T(1,128)} %gate.11), channel_id=1, source_target_pairs={{0,16},{8,24},{16,32},{24,40},{32,48},{40,56},{48,0},{56,8},{64,80... | collective-permute-start | bytes 1544 | tf_op jit(solution)/shard_map/ppermute | solution.py:390
  225.0 11.4 %collective-permute-done.18 = f32[1,128]{1,0:T(1,128)S(1)} collective-permute-done((f32[1,128]{1,0:T(1,128)}, f32[1,128]{1,0:T(1,128)S(1)}, u32[]{:S(2)}, u32[]{:S(2)}) %collective-permute-start.18) | collective-permute-done | bytes 544 | tf_op jit(solution)/shard_map/ppermute | solution.py:390
  236.4 6.6 %collective-permute-done.17 = f32[1,128]{1,0:T(1,128)S(1)} collective-permute-done((f32[1,128]{1,0:T(1,128)}, f32[1,128]{1,0:T(1,128)S(1)}, u32[]{:S(2)}, u32[]{:S(2)}) %collective-permute-start.17) | collective-permute-done | bytes 544 | tf_op jit(solution)/shard_map/ppermute | solution.py:390
  243.0 0.7 pad_maximum_fusion.5
  243.7 1.2 collective-permute-start.19
  245.0 0.7 copy.61
  245.7 3.5 %unpack.1 = (bf16[2,16,128,128]{3,2,1,0:T(8,128)(2,1)}, bf16[2,16,128,128]{3,2,1,0:T(8,128)(2,1)}) custom-call(s32[2,16]{1,0:T(2,128)} %copy-done.12, bf16[64,4,128,128]{3,2,1,0:T(8,128)(2,1)} %all-to-all-done.got_ref), custom_call_target="tpu_custom_call" | custom-call | bytes 4194304 | tf_op jit(solution)/shard_map/unpack/pallas_call | solution.py:89
  249.2 0.7 select_reduce_fusion
  (92 shorter events, 3.5 us)
Async XLA Ops:
  8.1 3.6 %collective-permute-start.2 = (bf16[32,8,128]{2,1,0:T(8,128)(2,1)S(1)}, bf16[32,8,128]{2,1,0:T(8,128)(2,1)S(1)}, u32[]{:S(2)}, u32[]{:S(2)}) collective-permute-start(bf16[32,8,128]{2,1,0:T(8,128)(2,1)S(1)} %get-tuple-element.56), channel_id=1, source_target_pairs={{248,184},{249,185},{250,186},{251,187},{252,188},{253,189},{254,1... | collective-permute-start | bytes 196616 | tf_op jit(solution)/shard_map/ppermute | solution.py:237
  8.8 3.0 %collective-permute-start = (bf16[32,8,128]{2,1,0:T(8,128)(2,1)S(1)}, bf16[32,8,128]{2,1,0:T(8,128)(2,1)S(1)}, u32[]{:S(2)}, u32[]{:S(2)}) collective-permute-start(bf16[32,8,128]{2,1,0:T(8,128)(2,1)S(1)} %get-tuple-element.57), channel_id=1, source_target_pairs={{248,56},{249,57},{250,58},{251,59},{252,60},{253,61},{254,62},{25... | collective-permute-start | bytes 196616 | tf_op jit(solution)/shard_map/ppermute | solution.py:237
  9.4 2.3 collective-permute-start.1
  10.8 9.1 %copy-start.9 = (s32[2,1,512]{2,0,1:T(2,128)}, s32[2,1,512]{2,0,1:T(2,128)S(1)}, u32[]{:S(2)}) copy-start(s32[2,1,512]{2,0,1:T(2,128)S(1)} %copy.76) | copy-start | bytes 12292
  12.6 2.8 %copy-start.1 = (bf16[32,8,128]{2,1,0:T(8,128)(2,1)}, bf16[32,8,128]{2,1,0:T(8,128)(2,1)S(1)}, u32[]{:S(2)}) copy-start(bf16[32,8,128]{2,1,0:T(8,128)(2,1)S(1)} %fusion.13.rest_0_) | copy-start | bytes 196612
  12.6 7.2 %collective-permute-start.5 = (bf16[32,8,128]{2,1,0:T(8,128)(2,1)S(1)}, bf16[32,8,128]{2,1,0:T(8,128)(2,1)S(1)}, u32[]{:S(2)}, u32[]{:S(2)}) collective-permute-start(bf16[32,8,128]{2,1,0:T(8,128)(2,1)S(1)} %fusion.13.rest_0_), channel_id=1, source_target_pairs={{56,40},{120,104},{184,168},{248,232},{57,41},{121,105},{185,169},... | collective-permute-start | bytes 196616 | tf_op jit(solution)/shard_map/ppermute | solution.py:243
  13.3 6.6 %collective-permute-start.3 = (bf16[32,8,128]{2,1,0:T(8,128)(2,1)S(1)}, bf16[32,8,128]{2,1,0:T(8,128)(2,1)S(1)}, u32[]{:S(2)}, u32[]{:S(2)}) collective-permute-start(bf16[32,8,128]{2,1,0:T(8,128)(2,1)S(1)} %fusion.13.rest_0_), channel_id=1, source_target_pairs={{56,8},{120,72},{184,136},{248,200},{57,9},{121,73},{185,137},{249... | collective-permute-start | bytes 196616 | tf_op jit(solution)/shard_map/ppermute | solution.py:243
  14.0 5.9 %collective-permute-start.4 = (bf16[32,8,128]{2,1,0:T(8,128)(2,1)S(1)}, bf16[32,8,128]{2,1,0:T(8,128)(2,1)S(1)}, u32[]{:S(2)}, u32[]{:S(2)}) collective-permute-start(bf16[32,8,128]{2,1,0:T(8,128)(2,1)S(1)} %fusion.13.rest_0_), channel_id=1, source_target_pairs={{56,24},{120,88},{184,152},{248,216},{57,25},{121,89},{185,153},{2... | collective-permute-start | bytes 196616 | tf_op jit(solution)/shard_map/ppermute | solution.py:243
  20.5 18.3 %collective-permute-start.6 = (bf16[32,8,128]{2,1,0:T(8,128)(2,1)}, bf16[32,8,128]{2,1,0:T(8,128)(2,1)S(1)}, u32[]{:S(2)}, u32[]{:S(2)}) collective-permute-start(bf16[32,8,128]{2,1,0:T(8,128)(2,1)} %gate.6.rest_0_), channel_id=1, source_target_pairs={{56,0},{8,16},{24,32},{40,48},{120,64},{72,80},{88,96},{104,112},{... | collective-permute-start | bytes 196616 | tf_op jit(solution)/shard_map/ppermute | solution.py:243
  21.9 17.0 %copy-start = (bf16[32,8,128]{2,1,0:T(8,128)(2,1)S(1)}, bf16[32,8,128]{2,1,0:T(8,128)(2,1)}, u32[]{:S(2)}) copy-start(bf16[32,8,128]{2,1,0:T(8,128)(2,1)} %gate.6.rest_0_) | copy-start | bytes 196612
  39.5 6.0 %collective-permute-start.8 = (bf16[32,8,128]{2,1,0:T(8,128)(2,1)}, bf16[32,8,128]{2,1,0:T(8,128)(2,1)S(1)}, u32[]{:S(2)}, u32[]{:S(2)}) collective-permute-start(bf16[32,8,128]{2,1,0:T(8,128)(2,1)} %gate.7), channel_id=1, source_target_pairs={{0,128},{8,136},{16,144},{24,152},{32,160},{40,168},{48,176},{56,1... | collective-permute-start | bytes 196616 | tf_op jit(solution)/shard_map/ppermute | solution.py:256
  39.5 6.0 %collective-permute-start.9 = (bf16[32,8,128]{2,1,0:T(8,128)(2,1)}, bf16[32,8,128]{2,1,0:T(8,128)(2,1)S(1)}, u32[]{:S(2)}, u32[]{:S(2)}) collective-permute-start(bf16[32,8,128]{2,1,0:T(8,128)(2,1)} %gate.7), channel_id=1, source_target_pairs={{0,192},{8,200},{16,208},{24,216},{32,224},{40,232},{48,240},{56,2... | collective-permute-start | bytes 196616 | tf_op jit(solution)/shard_map/ppermute | solution.py:256
  39.6 7.1 %collective-permute-start.7 = (bf16[32,8,128]{2,1,0:T(8,128)(2,1)}, bf16[32,8,128]{2,1,0:T(8,128)(2,1)S(1)}, u32[]{:S(2)}, u32[]{:S(2)}) collective-permute-start(bf16[32,8,128]{2,1,0:T(8,128)(2,1)} %gate.7), channel_id=1, source_target_pairs={{0,64},{8,72},{16,80},{24,88},{32,96},{40,104},{48,112},{56,120},{... | collective-permute-start | bytes 196616 | tf_op jit(solution)/shard_map/ppermute | solution.py:256
  45.5 1.2 copy-start.3
  45.5 1.2 copy-start.5
  46.7 0.6 copy-start.7
  47.3 9.5 %copy-start.2 = (bf16[32,8,128]{2,1,0:T(8,128)(2,1)S(1)}, bf16[32,8,128]{2,1,0:T(8,128)(2,1)}, u32[]{:S(2)}) copy-start(bf16[32,8,128]{2,1,0:T(8,128)(2,1)} %gate.7) | copy-start | bytes 196612
  47.3 9.5 %copy-start.4 = (bf16[32,8,128]{2,1,0:T(8,128)(2,1)S(1)}, bf16[32,8,128]{2,1,0:T(8,128)(2,1)}, u32[]{:S(2)}) copy-start(bf16[32,8,128]{2,1,0:T(8,128)(2,1)} %copy-done.3) | copy-start | bytes 196612
  47.3 9.5 %copy-start.6 = (bf16[32,8,128]{2,1,0:T(8,128)(2,1)S(1)}, bf16[32,8,128]{2,1,0:T(8,128)(2,1)}, u32[]{:S(2)}) copy-start(bf16[32,8,128]{2,1,0:T(8,128)(2,1)} %copy-done.5) | copy-start | bytes 196612
  47.3 9.5 %copy-start.8 = (bf16[32,8,128]{2,1,0:T(8,128)(2,1)S(1)}, bf16[32,8,128]{2,1,0:T(8,128)(2,1)}, u32[]{:S(2)}) copy-start(bf16[32,8,128]{2,1,0:T(8,128)(2,1)} %copy-done.7) | copy-start | bytes 196612
  47.4 196.3 %all-to-all-start = ((bf16[64,4,128,128]{3,2,1,0:T(8,128)(2,1)}), bf16[64,4,128,128]{3,2,1,0:T(8,128)(2,1)}, u32[]{:S(2)}, u32[]{:S(2)}) async-start(bf16[64,4,128,128]{3,2,1,0:T(8,128)(2,1)} %gate.10), calls=%async_computation | async-start | bytes 16777216 | tf_op jit(solution)/shard_map/all_to_all | solution.py:336
  55.3 117.6 %all-gather.3.cloned.1.call-start = ((), (), s32[]{:S(2)}) async-start(), calls=%async_computation.1 | async-start | bytes 1081344 | tf_op jit(solution)/shard_map/all_gather | solution.py:277
  57.6 19.7 %copy-start.11 = (s32[2,1,512]{2,1,0:T(1,128)S(1)}, s32[2,1,512]{2,1,0:T(1,128)}, u32[]{:S(2)}) copy-start(s32[2,1,512]{2,1,0:T(1,128)} %param.8) | copy-start | bytes 12292
  178.9 19.7 %copy-start.10 = (s32[2,64]{1,0:T(2,128)S(1)}, s32[2,64]{1,0:T(2,128)}, u32[]{:S(2)}) copy-start(s32[2,64]{1,0:T(2,128)} %reshape.385.index_ref) | copy-start | bytes 1540
  196.7 8.0 %collective-permute-start.10 = (f32[2,8192]{1,0:T(2,128)S(1)}, f32[2,8192]{1,0:T(2,128)S(1)}, u32[]{:S(2)}, u32[]{:S(2)}) collective-permute-start(f32[2,8192]{1,0:T(2,128)S(1)} %fusion.15), channel_id=1, source_target_pairs={{0,1},{1,0},{2,3},{3,2},{4,5},{5,4},{6,7},{7,6},{8,9},{9,8},{10,11... | collective-permute-start | bytes 196616 | tf_op jit(solution)/shard_map/ppermute | solution.py:292
  198.6 7.1 %collective-permute-start.15 = (f32[2,64]{1,0:T(2,128)S(1)}, f32[2,64]{1,0:T(2,128)S(1)}, u32[]{:S(2)}, u32[]{:S(2)}) collective-permute-start(f32[2,64]{1,0:T(2,128)S(1)} %fusion.28), channel_id=1, source_target_pairs={{0,192},{8,200},{16,208},{24,216},{32,224},{40,232},{48,240},{56,2... | collective-permute-start | bytes 1544 | tf_op jit(solution)/shard_map/ppermute | solution.py:376
  201.3 5.1 %collective-permute-start.14 = (f32[2,64]{1,0:T(2,128)S(1)}, f32[2,64]{1,0:T(2,128)S(1)}, u32[]{:S(2)}, u32[]{:S(2)}) collective-permute-start(f32[2,64]{1,0:T(2,128)S(1)} %fusion.28), channel_id=1, source_target_pairs={{0,128},{8,136},{16,144},{24,152},{32,160},{40,168},{48,176},{56,1... | collective-permute-start | bytes 1544 | tf_op jit(solution)/shard_map/ppermute | solution.py:376
  202.2 4.4 %collective-permute-start.13 = (f32[2,64]{1,0:T(2,128)S(1)}, f32[2,64]{1,0:T(2,128)S(1)}, u32[]{:S(2)}, u32[]{:S(2)}) collective-permute-start(f32[2,64]{1,0:T(2,128)S(1)} %fusion.28), channel_id=1, source_target_pairs={{0,64},{8,72},{16,80},{24,88},{32,96},{40,104},{48,112},{56,120},{... | collective-permute-start | bytes 1544 | tf_op jit(solution)/shard_map/ppermute | solution.py:376
  204.7 4.5 %collective-permute-start.11 = (f32[2,8192]{1,0:T(2,128)S(1)}, f32[2,8192]{1,0:T(2,128)S(1)}, u32[]{:S(2)}, u32[]{:S(2)}) collective-permute-start(f32[2,8192]{1,0:T(2,128)S(1)} %add.201), channel_id=1, source_target_pairs={{0,2},{1,3},{2,0},{3,1},{4,6},{5,7},{6,4},{7,5},{8,10},{9,11},{10,... | collective-permute-start | bytes 196616 | tf_op jit(solution)/shard_map/ppermute | solution.py:292
  209.3 5.9 %collective-permute-start.12 = (f32[2,8192]{1,0:T(2,128)S(1)}, f32[2,8192]{1,0:T(2,128)S(1)}, u32[]{:S(2)}, u32[]{:S(2)}) collective-permute-start(f32[2,8192]{1,0:T(2,128)S(1)} %add.202), channel_id=1, source_target_pairs={{0,4},{1,5},{2,6},{3,7},{4,0},{5,1},{6,2},{7,3},{8,12},{9,13},{10,... | collective-permute-start | bytes 196616 | tf_op jit(solution)/shard_map/ppermute | solution.py:292
  215.8 20.5 %collective-permute-start.18 = (f32[1,128]{1,0:T(1,128)}, f32[1,128]{1,0:T(1,128)S(1)}, u32[]{:S(2)}, u32[]{:S(2)}) collective-permute-start(f32[1,128]{1,0:T(1,128)} %gate.11), channel_id=1, source_target_pairs={{0,48},{8,56},{16,0},{24,8},{32,16},{40,24},{48,32},{56,40},{64,11... | collective-permute-start | bytes 1544 | tf_op jit(solution)/shard_map/ppermute | solution.py:390
  221.8 21.2 %collective-permute-start.17 = (f32[1,128]{1,0:T(1,128)}, f32[1,128]{1,0:T(1,128)S(1)}, u32[]{:S(2)}, u32[]{:S(2)}) collective-permute-start(f32[1,128]{1,0:T(1,128)} %gate.11), channel_id=1, source_target_pairs={{0,32},{8,40},{16,48},{24,56},{32,0},{40,8},{48,16},{56,24},{64,96... | collective-permute-start | bytes 1544 | tf_op jit(solution)/shard_map/ppermute | solution.py:390
  221.9 21.1 %collective-permute-start.16 = (f32[1,128]{1,0:T(1,128)}, f32[1,128]{1,0:T(1,128)S(1)}, u32[]{:S(2)}, u32[]{:S(2)}) collective-permute-start(f32[1,128]{1,0:T(1,128)} %gate.11), channel_id=1, source_target_pairs={{0,16},{8,24},{16,32},{24,40},{32,48},{40,56},{48,0},{56,8},{64,80... | collective-permute-start | bytes 1544 | tf_op jit(solution)/shard_map/ppermute | solution.py:390
  225.0 20.7 %copy-start.12 = (s32[2,16]{1,0:T(2,128)}, s32[2,16]{1,0:T(2,128)S(1)}, u32[]{:S(2)}) copy-start(s32[2,16]{1,0:T(2,128)S(1)} %select_reduce_fusion.3.index_ref) | copy-start | bytes 388
  243.7 5.5 %collective-permute-start.19 = (f32[4,128]{1,0:T(4,128)S(1)}, f32[4,128]{1,0:T(4,128)S(1)}, u32[]{:S(2)}, u32[]{:S(2)}) collective-permute-start(f32[4,128]{1,0:T(4,128)S(1)} %pad_maximum_fusion.5), channel_id=1, source_target_pairs={{0,8},{8,16},{16,24},{24,32},{32,40},{40,48},{48,56},{56,0},{64,72... | collective-permute-start | bytes 6152 | tf_op jit(solution)/shard_map/ppermute | solution.py:390
Sparse Core Ops, SparseCore 0:
  77.5 95.3 all-gather.2
